TPU v7x, 512 devices: a whole 4x4x16 slice. The times are simulated.
512 devices in a mesh: image: 32 (over z, core), band: 16 (over y, x).
Axes of the slice: x: 4, y: 4, z: 16, core: 2. Of those that a mesh axis runs over, the one named last changes fastest.
Arguments:
- images: float32 [32, 128, 64, 128], P('image', None, 'band'), may hold values from -60 to 60, as said below
- cotangent: float32 [32, 128, 64, 128], P('image', None, 'band'), may hold values from -6 to 6
- filters: float32 [2, 1152, 128], replicated, may hold values from -6 to 6
- rates: float32 [2], replicated, may hold values from 0.002 to 0.008
Outputs:
- new_filters: float32 [32, 2, 1152, 128], P('image')
Inputs may be any that keep to these rules, and one draw needn't show every extreme that they name: `images`: Real-valued feature maps whose channels differ in scale.
All inputs are finite; a program needn't handle non-finite values.
Results may differ from a plain program's by a relative error of at most 0.0001.
Values sent between devices are 32-bit elements; how exact they have to be, the bound alone decides.
A program may use at most 64 MiB of HBM per device.

v0:
```python
import jax
import jax.numpy as jnp
from jax import lax
from jax.sharding import PartitionSpec as P

HIGH = lax.Precision.HIGHEST


def extended_2(block, sides, width):
    for axis, dim in sides:
        count = lax.axis_size(axis)
        forward = [(i, i + 1) for i in range(count - 1)]
        backward = [(target, source) for source, target in forward]
        low = lax.ppermute(
            lax.slice_in_dim(block, block.shape[dim] - width, None, axis=dim), axis, forward
        )
        high = lax.ppermute(lax.slice_in_dim(block, 0, width, axis=dim), axis, backward)
        block = jnp.concatenate([low, block, high], axis=dim)
    return block


def split_up(shard, dim, count):
    dims = shard.shape
    blocks = shard.reshape(*dims[:dim], count, dims[dim] // count, *dims[dim + 1 :])
    return jnp.moveaxis(blocks, dim, 0)


def sum_at_owner(shard, axis, dim):
    count = lax.axis_size(axis)
    blocks = lax.all_to_all(split_up(shard, dim, count), axis, 0, 0, tiled=True)
    return jnp.sum(blocks, axis=0)


def partner(block, axis, apart):
    count = lax.axis_size(axis)
    route = []
    for low in range(count):
        high = low | 1 << apart
        if high != low and high < count:
            route += [(low, high), (high, low)]
    return lax.ppermute(block, axis, route)


def from_everyone(shard, axis):
    copies = jnp.broadcast_to(shard, (lax.axis_size(axis), *shard.shape))
    return lax.all_to_all(copies, axis, split_axis=0, concat_axis=0, tiled=True)


def taken_together(shard, axis):
    return from_everyone(shard, axis).sum(axis=0)


def in_one(arrays, axis):
    ravelled, at, done = (jnp.concatenate([a.reshape(-1) for a in arrays]), 0, [])
    total = taken_together(ravelled, axis)
    for a in arrays:
        done.append(total[at : at + a.size].reshape(a.shape))
        at += a.size
    return tuple(done)


def joined_along(blocks, dim):
    dims = list(blocks.shape[1:])
    dims[dim] *= blocks.shape[0]
    return jnp.moveaxis(blocks, 0, dim).reshape(dims)


def collect(shard, axis, dim):
    return joined_along(from_everyone(shard, axis), dim)


def taps(padded, rows, cols):
    chans = padded.shape[0]
    pieces = [padded[:, dr : dr + rows, dc : dc + cols] for dr in range(3) for dc in range(3)]
    return jnp.stack(pieces, axis=1).reshape(chans * 9, rows * cols)


def flipped(padded, rows, cols):
    chans = padded.shape[0]
    pieces = [
        padded[:, 2 - dr : 2 - dr + rows, 2 - dc : 2 - dc + cols]
        for dr in range(3)
        for dc in range(3)
    ]
    return jnp.stack(pieces, axis=1).reshape(chans, 9, rows * cols)


def with_rims(field):
    extended = extended_2(field, (("band", 1),), 1)
    return jnp.pad(extended, ((0, 0), (0, 0), (1, 1)))


def combine(own, other, inner, own_sq, other_sq):
    coef_own = (1.0 - inner / (2.0 * (own_sq + 1e-06)))[:, None, None]
    coef_other = (1.0 - inner / (2.0 * (other_sq + 1e-06)))[:, None, None]
    return coef_own * own + coef_other * other


def local(images, cotangent, filters, rates):
    feats = images[0]
    cot = cotangent[0]
    chans = feats.shape[0]
    rows = feats.shape[1]
    cols = feats.shape[2]
    scale = (9 * chans) ** (-0.5)
    patch_one = taps(with_rims(feats), rows, cols)
    pre = scale * jnp.einsum("kc,kp->cp", filters[0], patch_one, precision=HIGH)
    hidden = jax.nn.silu(pre).reshape(chans, rows, cols)
    patch_two = taps(with_rims(hidden), rows, cols)
    back = flipped(with_rims(cot), rows, cols)
    flat_cot = cot.reshape(chans, rows * cols)
    grad_two = scale * jnp.einsum("kp,cp->kc", patch_two, flat_cot, precision=HIGH)
    weight_two = filters[1].reshape(chans, 9, chans)
    dhidden = scale * jnp.einsum("itc,ctp->ip", weight_two, back, precision=HIGH)
    sig = jax.nn.sigmoid(pre)
    dpre = dhidden * sig * (1.0 + pre * (1.0 - sig))
    grad_one = scale * jnp.einsum("kp,cp->kc", patch_one, dpre, precision=HIGH)
    grads = jnp.stack([grad_one, grad_two])
    levels = lax.axis_size("image").bit_length() - 1
    block = sum_at_owner(grads, "band", 1)
    for level in range(levels):
        other = partner(block, "image", level)
        inner, own_sq, other_sq = in_one(
            (
                jnp.sum(block * other, axis=(1, 2)),
                jnp.sum(block * block, axis=(1, 2)),
                jnp.sum(other * other, axis=(1, 2)),
            ),
            "band",
        )
        block = combine(block, other, inner, own_sq, other_sq)
    height = block.shape[1]
    start = lax.axis_index("band") * height
    mine = lax.dynamic_slice_in_dim(filters, start, height, 1)
    fresh = (mine - rates[:, None, None] * block)[None]
    return collect(fresh, "band", 2)


def solution(mesh):
    in_specs = (P("image", None, "band", None), P("image", None, "band", None), P(), P())
    out_specs = P("image", None, None, None)
    return jax.shard_map(local, mesh=mesh, in_specs=in_specs, out_specs=out_specs, check_vma=False)
```

profile of v0, /device:TPU:2, one launch (start us, length us, event | category | flops | bytes accessed | tf_op | source)
XLA Modules:
  0.0 212.0 jit_solution(12005918709928989316)
XLA Ops:
  1.2 3.4 %collective-permute-start.2 = (f32[128,1,128]{2,1,0:T(1,128)S(1)}, f32[128,1,128]{2,1,0:T(1,128)S(1)}, u32[]{:S(2)}, u32[]{:S(2)}) collective-permute-start(f32[128,1,128]{2,1,0:T(1,128)S(1)} %get-tuple-element.28), channel_id=1, source_target_pairs={{0,1},{1,2},{2,3},{3,4},{4,5},{5,6},{6,7},{7,8},{8,9},{9,10},{10,1... | collective-permute-start | bytes 196616 | tf_op jit(solution)/shard_map/ppermute | solution.py:14
  4.6 5.7 %collective-permute-start.3 = (f32[128,1,128]{2,1,0:T(1,128)S(1)}, f32[128,1,128]{2,1,0:T(1,128)S(1)}, u32[]{:S(2)}, u32[]{:S(2)}) collective-permute-start(f32[128,1,128]{2,1,0:T(1,128)S(1)} %get-tuple-element.29), channel_id=1, source_target_pairs={{1,0},{2,1},{3,2},{4,3},{5,4},{6,5},{7,6},{8,7},{9,8},{10,9},{11,1... | collective-permute-start | bytes 196616 | tf_op jit(solution)/shard_map/ppermute | solution.py:17
  13.4 3.9 %collective-permute-start.1 = (f32[128,1,128]{2,1,0:T(1,128)S(1)}, f32[128,1,128]{2,1,0:T(1,128)S(1)}, u32[]{:S(2)}, u32[]{:S(2)}) collective-permute-start(f32[128,1,128]{2,1,0:T(1,128)S(1)} %get-tuple-element.33), channel_id=1, source_target_pairs={{1,0},{2,1},{3,2},{4,3},{5,4},{6,5},{7,6},{8,7},{9,8},{10,9},{11,1... | collective-permute-start | bytes 196616 | tf_op jit(solution)/shard_map/ppermute | solution.py:17
  32.2 4.6 %fusion.43 = (f32[128,512]{0,1:T(8,128)S(1)}, f32[128,512]{0,1:T(8,128)}) fusion(f32[2,1152,128]{2,1,0:T(8,128)S(1)} %copy-done.3, f32[144,8,4,128]{3,2,1,0:T(4,128)S(1)} %bitcast.164), kind=kOutput, calls=%fused_computation.79 | convolution fusion | flops 906297344 | bytes 3473408 | tf_op jit(solution)/shard_map/kc,kp->cp/dot_general | solution.py:107
  39.7 4.7 %collective-permute-start.5 = (f32[128,1,128]{2,1,0:T(1,128)}, f32[128,1,128]{2,1,0:T(1,128)S(1)}, u32[]{:S(2)}, u32[]{:S(2)}) collective-permute-start(f32[128,1,128]{2,1,0:T(1,128)} %get-tuple-element.31), channel_id=1, source_target_pairs={{1,0},{2,1},{3,2},{4,3},{5,4},{6,5},{7,6},{8,7},{9,8},{10,9},{11,1... | collective-permute-start | bytes 196616 | tf_op jit(solution)/shard_map/ppermute | solution.py:17
  53.1 3.9 %fusion.16 = f32[128,512]{0,1:T(8,128)S(1)} fusion(f32[128,9,512]{0,2,1:T(8,128)} %bitcast_dynamic-update-slice_fusion, f32[128,9,128]{2,1,0:T(8,128)S(1)} %copy-done.2, f32[128,512]{0,1:T(8,128)S(1)} %copy-done.11), kind=kOutput, calls=%fused_computation.18 | convolution fusion | flops 906559488 | bytes 3473408 | tf_op jit(solution)/shard_map/itc,ctp->ip/dot_general | solution.py:114
  57.0 2.0 convolution_multiply_fusion.1
  64.2 2.0 convolution_multiply_fusion
  66.4 23.0 %all_to_all.40 = f32[16,2,72,128]{3,2,1,0:T(8,128)S(1)} all-to-all(f32[16,2,72,128]{3,2,1,0:T(8,128)S(1)} %maximum_bitcast_fusion), channel_id=1, replica_groups=mesh['image'=32,'band'=16] {'band'}, dimensions={0} | all-to-all | bytes 2359296 | tf_op jit(solution)/shard_map/all_to_all | solution.py:30
  92.7 10.6 %all_to_all.41 = f32[16,1,6]{2,1,0:T(1,128)S(1)} all-to-all(f32[16,1,6]{2,1,0:T(1,128)S(1)} %broadcast_in_dim.12), channel_id=1, replica_groups=mesh['image'=32,'band'=16] {'band'}, dimensions={0} | all-to-all | bytes 768 | tf_op jit(solution)/shard_map/all_to_all | solution.py:46
  103.6 3.8 %collective-permute-start.7 = (f32[2,72,128]{2,1,0:T(8,128)S(1)}, f32[2,72,128]{2,1,0:T(8,128)S(1)}, u32[]{:S(2)}, u32[]{:S(2)}) collective-permute-start(f32[2,72,128]{2,1,0:T(8,128)S(1)} %multiply_add_fusion.3), channel_id=1, source_target_pairs={{0,32},{32,0},{16,48},{48,16},{64,96},{96,64},{80,112},{112,80},{1... | collective-permute-start | bytes 221192 | tf_op jit(solution)/shard_map/ppermute | solution.py:41
  107.4 2.4 %collective-permute-done.7 = f32[2,72,128]{2,1,0:T(8,128)S(1)} collective-permute-done((f32[2,72,128]{2,1,0:T(8,128)S(1)}, f32[2,72,128]{2,1,0:T(8,128)S(1)}, u32[]{:S(2)}, u32[]{:S(2)}) %collective-permute-start.7) | collective-permute-done | bytes 73760 | tf_op jit(solution)/shard_map/ppermute | solution.py:41
  110.0 10.5 %all_to_all.42 = f32[16,1,6]{2,1,0:T(1,128)S(1)} all-to-all(f32[16,1,6]{2,1,0:T(1,128)S(1)} %broadcast_in_dim.13), channel_id=1, replica_groups=mesh['image'=32,'band'=16] {'band'}, dimensions={0} | all-to-all | bytes 768 | tf_op jit(solution)/shard_map/all_to_all | solution.py:46
  120.8 5.2 %collective-permute-start.8 = (f32[2,72,128]{2,1,0:T(8,128)S(1)}, f32[2,72,128]{2,1,0:T(8,128)S(1)}, u32[]{:S(2)}, u32[]{:S(2)}) collective-permute-start(f32[2,72,128]{2,1,0:T(8,128)S(1)} %multiply_add_fusion.2), channel_id=1, source_target_pairs={{0,64},{64,0},{16,80},{80,16},{32,96},{96,32},{48,112},{112,48},{1... | collective-permute-start | bytes 221192 | tf_op jit(solution)/shard_map/ppermute | solution.py:41
  126.0 2.3 %collective-permute-done.8 = f32[2,72,128]{2,1,0:T(8,128)S(1)} collective-permute-done((f32[2,72,128]{2,1,0:T(8,128)S(1)}, f32[2,72,128]{2,1,0:T(8,128)S(1)}, u32[]{:S(2)}, u32[]{:S(2)}) %collective-permute-start.8) | collective-permute-done | bytes 73760 | tf_op jit(solution)/shard_map/ppermute | solution.py:41
  128.5 10.5 %all_to_all.43 = f32[16,1,6]{2,1,0:T(1,128)S(1)} all-to-all(f32[16,1,6]{2,1,0:T(1,128)S(1)} %broadcast_in_dim.14), channel_id=1, replica_groups=mesh['image'=32,'band'=16] {'band'}, dimensions={0} | all-to-all | bytes 768 | tf_op jit(solution)/shard_map/all_to_all | solution.py:46
  139.2 9.1 %collective-permute-start.9 = (f32[2,72,128]{2,1,0:T(8,128)S(1)}, f32[2,72,128]{2,1,0:T(8,128)S(1)}, u32[]{:S(2)}, u32[]{:S(2)}) collective-permute-start(f32[2,72,128]{2,1,0:T(8,128)S(1)} %multiply_add_fusion.1), channel_id=1, source_target_pairs={{0,128},{128,0},{16,144},{144,16},{32,160},{160,32},{48,176},{176,... | collective-permute-start | bytes 221192 | tf_op jit(solution)/shard_map/ppermute | solution.py:41
  148.3 2.3 %collective-permute-done.9 = f32[2,72,128]{2,1,0:T(8,128)S(1)} collective-permute-done((f32[2,72,128]{2,1,0:T(8,128)S(1)}, f32[2,72,128]{2,1,0:T(8,128)S(1)}, u32[]{:S(2)}, u32[]{:S(2)}) %collective-permute-start.9) | collective-permute-done | bytes 73760 | tf_op jit(solution)/shard_map/ppermute | solution.py:41
  150.8 10.5 %all_to_all.44 = f32[16,1,6]{2,1,0:T(1,128)S(1)} all-to-all(f32[16,1,6]{2,1,0:T(1,128)S(1)} %broadcast_in_dim.15), channel_id=1, replica_groups=mesh['image'=32,'band'=16] {'band'}, dimensions={0} | all-to-all | bytes 768 | tf_op jit(solution)/shard_map/all_to_all | solution.py:46
  161.6 17.0 %collective-permute-start.10 = (f32[2,72,128]{2,1,0:T(8,128)S(1)}, f32[2,72,128]{2,1,0:T(8,128)S(1)}, u32[]{:S(2)}, u32[]{:S(2)}) collective-permute-start(f32[2,72,128]{2,1,0:T(8,128)S(1)} %multiply_add_fusion), channel_id=1, source_target_pairs={{0,256},{256,0},{16,272},{272,16},{32,288},{288,32},{48,304},{304,... | collective-permute-start | bytes 221192 | tf_op jit(solution)/shard_map/ppermute | solution.py:41
  178.6 2.3 %collective-permute-done.10 = f32[2,72,128]{2,1,0:T(8,128)S(1)} collective-permute-done((f32[2,72,128]{2,1,0:T(8,128)S(1)}, f32[2,72,128]{2,1,0:T(8,128)S(1)}, u32[]{:S(2)}, u32[]{:S(2)}) %collective-permute-start.10) | collective-permute-done | bytes 73760 | tf_op jit(solution)/shard_map/ppermute | solution.py:41
  181.7 4.7 %all-to-all-start.5 = ((f32[16,1,6]{2,1,0:T(1,128)}), f32[16,1,6]{2,1,0:T(1,128)S(1)}, u32[]{:S(2)}, u32[]{:S(2)}) async-start(f32[16,1,6]{2,1,0:T(1,128)} %broadcast_in_dim.16), calls=%async_computation.5 | async-start | bytes 16384 | tf_op jit(solution)/shard_map/all_to_all | solution.py:46
  186.4 6.2 %all-to-all-done.5 = f32[16,1,6]{2,1,0:T(1,128)S(1)} async-done(((f32[16,1,6]{2,1,0:T(1,128)}), f32[16,1,6]{2,1,0:T(1,128)S(1)}, u32[]{:S(2)}, u32[]{:S(2)}) %all-to-all-start.5) | async-done | bytes 416 | tf_op jit(solution)/shard_map/all_to_all | solution.py:46
  193.0 17.9 %all_to_all.45 = f32[16,1,2,72,128]{4,3,2,1,0:T(8,128)S(1)} all-to-all(f32[16,1,2,72,128]{4,3,2,1,0:T(8,128)S(1)} %broadcast_in_dim.17), channel_id=1, replica_groups=mesh['image'=32,'band'=16] {'band'}, dimensions={0} | all-to-all | bytes 2359296 | tf_op jit(solution)/shard_map/all_to_all | solution.py:46
  (120 shorter events, 42.8 us)
Async XLA Ops:
  0.0 20.2 %copy-start = (f32[1,128,4,128]{3,2,1,0:T(4,128)S(1)}, f32[1,128,4,128]{3,2,1,0:T(4,128)}, u32[]{:S(2)}) copy-start(f32[1,128,4,128]{3,2,1,0:T(4,128)} %param.5) | copy-start | bytes 786436
  0.0 19.1 %slice-start = ((f32[2,1152,128]{2,1,0:T(8,128)}), f32[1,1152,128]{2,1,0:T(8,128)S(1)}, s32[]{:S(2)}) async-start(f32[2,1152,128]{2,1,0:T(8,128)} %param.6), calls=%async_computation.7 | async-start | bytes 1179648 | tf_op jit(solution)/shard_map/slice | solution.py:113
  1.2 19.0 %collective-permute-start.2 = (f32[128,1,128]{2,1,0:T(1,128)S(1)}, f32[128,1,128]{2,1,0:T(1,128)S(1)}, u32[]{:S(2)}, u32[]{:S(2)}) collective-permute-start(f32[128,1,128]{2,1,0:T(1,128)S(1)} %get-tuple-element.28), channel_id=1, source_target_pairs={{0,1},{1,2},{2,3},{3,4},{4,5},{5,6},{6,7},{7,8},{8,9},{9,10},{10,1... | collective-permute-start | bytes 196616 | tf_op jit(solution)/shard_map/ppermute | solution.py:14
  4.6 15.6 %collective-permute-start.3 = (f32[128,1,128]{2,1,0:T(1,128)S(1)}, f32[128,1,128]{2,1,0:T(1,128)S(1)}, u32[]{:S(2)}, u32[]{:S(2)}) collective-permute-start(f32[128,1,128]{2,1,0:T(1,128)S(1)} %get-tuple-element.29), channel_id=1, source_target_pairs={{1,0},{2,1},{3,2},{4,3},{5,4},{6,5},{7,6},{8,7},{9,8},{10,9},{11,1... | collective-permute-start | bytes 196616 | tf_op jit(solution)/shard_map/ppermute | solution.py:17
  11.5 17.1 %collective-permute-start = (f32[128,1,128]{2,1,0:T(1,128)S(1)}, f32[128,1,128]{2,1,0:T(1,128)S(1)}, u32[]{:S(2)}, u32[]{:S(2)}) collective-permute-start(f32[128,1,128]{2,1,0:T(1,128)S(1)} %get-tuple-element.32), channel_id=1, source_target_pairs={{0,1},{1,2},{2,3},{3,4},{4,5},{5,6},{6,7},{7,8},{8,9},{9,10},{10,1... | collective-permute-start | bytes 196616 | tf_op jit(solution)/shard_map/ppermute | solution.py:14
  13.4 15.2 %collective-permute-start.1 = (f32[128,1,128]{2,1,0:T(1,128)S(1)}, f32[128,1,128]{2,1,0:T(1,128)S(1)}, u32[]{:S(2)}, u32[]{:S(2)}) collective-permute-start(f32[128,1,128]{2,1,0:T(1,128)S(1)} %get-tuple-element.33), channel_id=1, source_target_pairs={{1,0},{2,1},{3,2},{4,3},{5,4},{6,5},{7,6},{8,7},{9,8},{10,9},{11,1... | collective-permute-start | bytes 196616 | tf_op jit(solution)/shard_map/ppermute | solution.py:17
  32.2 17.2 %copy-start.6 = (f32[1,128,4,128]{1,3,2,0:T(8,128)S(1)}, f32[1,128,4,128]{1,3,2,0:T(8,128)}, u32[]{:S(2)}) copy-start(f32[1,128,4,128]{1,3,2,0:T(8,128)} %copy.126) | copy-start | bytes 786436
  36.8 16.3 %copy-start.5 = (f32[128,512]{0,1:T(8,128)}, f32[128,512]{0,1:T(8,128)S(1)}, u32[]{:S(2)}) copy-start(f32[128,512]{0,1:T(8,128)S(1)} %get-tuple-element.44) | copy-start | bytes 786436
  37.0 13.2 %copy-start.10 = (f32[128,4,128]{0,2,1:T(8,128)S(1)}, f32[128,4,128]{0,2,1:T(8,128)}, u32[]{:S(2)}) copy-start(f32[128,4,128]{0,2,1:T(8,128)} %copy.127) | copy-start | bytes 786436
  37.0 13.9 %copy-start.9 = (f32[128,4,128]{0,2,1:T(8,128)S(1)}, f32[128,4,128]{0,2,1:T(8,128)}, u32[]{:S(2)}) copy-start(f32[128,4,128]{0,2,1:T(8,128)} %copy.128) | copy-start | bytes 786436
  37.0 14.6 %copy-start.7 = (f32[128,4,128]{0,2,1:T(8,128)S(1)}, f32[128,4,128]{0,2,1:T(8,128)}, u32[]{:S(2)}) copy-start(f32[128,4,128]{0,2,1:T(8,128)} %copy.129) | copy-start | bytes 786436
  37.0 15.3 %copy-start.8 = (f32[128,4,128]{0,2,1:T(8,128)S(1)}, f32[128,4,128]{0,2,1:T(8,128)}, u32[]{:S(2)}) copy-start(f32[128,4,128]{0,2,1:T(8,128)} %copy.130) | copy-start | bytes 786436
  37.0 16.1 %copy-start.2 = (f32[128,9,128]{2,1,0:T(8,128)S(1)}, f32[128,9,128]{2,1,0:T(8,128)}, u32[]{:S(2)}) copy-start(f32[128,9,128]{2,1,0:T(8,128)} %reshape_squeeze.6) | copy-start | bytes 1769476
  37.0 16.1 %copy-start.11 = (f32[128,512]{0,1:T(8,128)S(1)}, f32[128,512]{0,1:T(8,128)}, u32[]{:S(2)}) copy-start(f32[128,512]{0,1:T(8,128)} %get-tuple-element.45) | copy-start | bytes 786436
  37.8 22.4 %collective-permute-start.4 = (f32[128,1,128]{2,1,0:T(1,128)}, f32[128,1,128]{2,1,0:T(1,128)}, u32[]{:S(2)}, u32[]{:S(2)}) collective-permute-start(f32[128,1,128]{2,1,0:T(1,128)} %get-tuple-element.30), channel_id=1, source_target_pairs={{0,1},{1,2},{2,3},{3,4},{4,5},{5,6},{6,7},{7,8},{8,9},{9,10},{10,1... | collective-permute-start | bytes 196616 | tf_op jit(solution)/shard_map/ppermute | solution.py:14
  39.7 20.4 %collective-permute-start.5 = (f32[128,1,128]{2,1,0:T(1,128)}, f32[128,1,128]{2,1,0:T(1,128)S(1)}, u32[]{:S(2)}, u32[]{:S(2)}) collective-permute-start(f32[128,1,128]{2,1,0:T(1,128)} %get-tuple-element.31), channel_id=1, source_target_pairs={{1,0},{2,1},{3,2},{4,3},{5,4},{6,5},{7,6},{8,7},{9,8},{10,9},{11,1... | collective-permute-start | bytes 196616 | tf_op jit(solution)/shard_map/ppermute | solution.py:17
  66.3 126.5 %copy-start.4 = (f32[2,1152,128]{2,1,0:T(8,128)S(1)}, f32[2,1152,128]{2,1,0:T(8,128)}, u32[]{:S(2)}) copy-start(f32[2,1152,128]{2,1,0:T(8,128)} %param.6) | copy-start | bytes 3538948
  66.3 126.5 %copy-start.12 = (f32[2]{0:T(128)S(1)}, f32[2]{0:T(128)}, u32[]{:S(2)}) copy-start(f32[2]{0:T(128)} %param.7) | copy-start | bytes 28
  89.4 3.2 %collective-permute-start.6 = (f32[2,72,128]{2,1,0:T(8,128)S(1)}, f32[2,72,128]{2,1,0:T(8,128)S(1)}, u32[]{:S(2)}, u32[]{:S(2)}) collective-permute-start(f32[2,72,128]{2,1,0:T(8,128)S(1)} %reduce_sum.189), channel_id=1, source_target_pairs={{0,16},{16,0},{32,48},{48,32},{64,80},{80,64},{96,112},{112,96},{1... | collective-permute-start | bytes 221192 | tf_op jit(solution)/shard_map/ppermute | solution.py:41
  103.6 6.2 %collective-permute-start.7 = (f32[2,72,128]{2,1,0:T(8,128)S(1)}, f32[2,72,128]{2,1,0:T(8,128)S(1)}, u32[]{:S(2)}, u32[]{:S(2)}) collective-permute-start(f32[2,72,128]{2,1,0:T(8,128)S(1)} %multiply_add_fusion.3), channel_id=1, source_target_pairs={{0,32},{32,0},{16,48},{48,16},{64,96},{96,64},{80,112},{112,80},{1... | collective-permute-start | bytes 221192 | tf_op jit(solution)/shard_map/ppermute | solution.py:41
  120.8 7.5 %collective-permute-start.8 = (f32[2,72,128]{2,1,0:T(8,128)S(1)}, f32[2,72,128]{2,1,0:T(8,128)S(1)}, u32[]{:S(2)}, u32[]{:S(2)}) collective-permute-start(f32[2,72,128]{2,1,0:T(8,128)S(1)} %multiply_add_fusion.2), channel_id=1, source_target_pairs={{0,64},{64,0},{16,80},{80,16},{32,96},{96,32},{48,112},{112,48},{1... | collective-permute-start | bytes 221192 | tf_op jit(solution)/shard_map/ppermute | solution.py:41
  139.2 11.4 %collective-permute-start.9 = (f32[2,72,128]{2,1,0:T(8,128)S(1)}, f32[2,72,128]{2,1,0:T(8,128)S(1)}, u32[]{:S(2)}, u32[]{:S(2)}) collective-permute-start(f32[2,72,128]{2,1,0:T(8,128)S(1)} %multiply_add_fusion.1), channel_id=1, source_target_pairs={{0,128},{128,0},{16,144},{144,16},{32,160},{160,32},{48,176},{176,... | collective-permute-start | bytes 221192 | tf_op jit(solution)/shard_map/ppermute | solution.py:41
  161.6 19.3 %collective-permute-start.10 = (f32[2,72,128]{2,1,0:T(8,128)S(1)}, f32[2,72,128]{2,1,0:T(8,128)S(1)}, u32[]{:S(2)}, u32[]{:S(2)}) collective-permute-start(f32[2,72,128]{2,1,0:T(8,128)S(1)} %multiply_add_fusion), channel_id=1, source_target_pairs={{0,256},{256,0},{16,272},{272,16},{32,288},{288,32},{48,304},{304,... | collective-permute-start | bytes 221192 | tf_op jit(solution)/shard_map/ppermute | solution.py:41
  181.7 11.0 %all-to-all-start.5 = ((f32[16,1,6]{2,1,0:T(1,128)}), f32[16,1,6]{2,1,0:T(1,128)S(1)}, u32[]{:S(2)}, u32[]{:S(2)}) async-start(f32[16,1,6]{2,1,0:T(1,128)} %broadcast_in_dim.16), calls=%async_computation.5 | async-start | bytes 16384 | tf_op jit(solution)/shard_map/all_to_all | solution.py:46
  (2 other events, 6.4 us)
where the time goes:
time: 213 us; the launch traced here: 212 us
  blocking collectives  83.1 us (39%)
  starting transfers between devices  63.3 us (30%)
  local copies, waits for them, and re-layouts  28.4 us (13%)
  waiting for transfers between devices  16.8 us (8%)
  matrix products  12.5 us (6%)
  other arithmetic  7.33 us (3%)
    all_to_all x5, blocking collectives, from_everyone(): return lax.all_to_all(copies, axis, split_axis=0, concat_axis=0, tiled=True)  60.1 us
    ppermute x5, starting transfers between devices, partner(): return lax.ppermute(block, axis, route)  37.1 us
    all_to_all x1, blocking collectives, sum_at_owner(): blocks = lax.all_to_all(split_up(shard, dim, count), axis, 0, 0, tiled=True)  23 us
    ppermute x3, starting transfers between devices, extended_2(): lax.ppermute(lax.slice_in_dim(block, 0, width, axis=dim), axis, backward)  14.3 us
    unnamed x47, local copies, waits for them, and re-layouts  13 us
    ppermute x5, waiting for transfers between devices, partner(): return lax.ppermute(block, axis, route)  10.6 us
    ppermute x3, starting transfers between devices, extended_2(): lax.ppermute(lax.slice_in_dim(block, block.shape[dim] - width, None, axis...  7.23 us
    slice x9, local copies, waits for them, and re-layouts, flipped(): padded[:, 2 - dr:2 - dr + rows, 2 - dc:2 - dc + cols]  6.56 us
  transfers between devices with their start and end apart: 12, of which 6 were waited for; matrix products, arithmetic and copies ran while one was open for 13% of the time, Pallas kernels for 0%

commit v1 on v0

v1 whole, which is shorter than its diff:
```python
import functools

import jax
import jax.numpy as jnp
from jax import lax
from jax.experimental import pallas as pl
from jax.experimental.pallas import tpu as pltpu
from jax.sharding import PartitionSpec as P

MESH = pl.DeviceIdType.MESH
F32 = jnp.float32
BF16 = jnp.bfloat16
HIGH = lax.Precision.HIGHEST


def remote(src, dst, send, recv, image, band):
    return pltpu.make_async_remote_copy(
        src_ref=src,
        dst_ref=dst,
        send_sem=send,
        recv_sem=recv,
        device_id={"image": image, "band": band},
        device_id_type=MESH,
    )


def halves(v):
    hi = v.astype(BF16)
    return hi, (v - hi.astype(F32)).astype(BF16)


def before(v):
    lane = lax.broadcasted_iota(jnp.int32, v.shape, 1)
    return jnp.where(lane == 0, 0.0, pltpu.roll(v, 1, 1))


def after(v):
    lane = lax.broadcasted_iota(jnp.int32, v.shape, 1)
    return jnp.where(lane == 127, 0.0, pltpu.roll(v, 127, 1))


def nn(a, b):
    return lax.dot_general(a, b, (((1,), (0,)), ((), ())), preferred_element_type=F32)


def nt(a, b):
    return lax.dot_general(a, b, (((1,), (1,)), ((), ())), preferred_element_type=F32)


def partner_sum(h, level):
    bit = 1 << level
    row = lax.broadcasted_iota(jnp.int32, h.shape, 0)
    if bit >= 8:
        blocks = [h[8 * k : 8 * k + 8] for k in range(4)]
        other = jnp.concatenate([blocks[k ^ (bit // 8)] for k in range(4)], axis=0)
    else:
        blocks = []
        for k in range(4):
            v = h[8 * k : 8 * k + 8]
            r = lax.broadcasted_iota(jnp.int32, v.shape, 0)
            blocks.append(jnp.where((r & bit) == 0, pltpu.roll(v, 8 - bit, 0), pltpu.roll(v, bit, 0)))
        other = jnp.concatenate(blocks, axis=0)
    h = h + other
    lane = lax.broadcasted_iota(jnp.int32, h.shape, 1)
    other = jnp.where((lane & bit) == 0, pltpu.roll(h, 128 - bit, 1), pltpu.roll(h, bit, 1))
    return h + other


def adasum_weights(gram):
    row = lax.broadcasted_iota(jnp.int32, gram.shape, 0)
    lane = lax.broadcasted_iota(jnp.int32, gram.shape, 1)
    alpha = jnp.ones((32, 1), F32)
    for level in range(5):
        own = row == lane
        pair = row == (lane ^ (1 << level))
        sq = jnp.where(own, gram, 0.0)
        inner = jnp.where(pair, gram, 0.0)
        u_col = 1.0 - jnp.sum(inner, axis=1, keepdims=True) / (
            2.0 * (jnp.sum(sq, axis=1, keepdims=True) + 1e-6)
        )
        alpha = alpha * u_col
        if level < 4:
            u_row = 1.0 - jnp.sum(inner, axis=0, keepdims=True) / (
                2.0 * (jnp.sum(sq, axis=0, keepdims=True) + 1e-6)
            )
            gram = partner_sum(gram * u_col * u_row, level)
    return alpha


def kernel(
    img, cot, fil, rates, out,
    xbuf, ybuf, xh, xl, yh, yl, w1h, w1l, w2h, w2l, z, dsig, hh, hl,
    ga, gb, oppa, oppb, rawa, rawb, suma, sumb, stage_a, stage_b, lata, latb, sown,
    tiles, gram_z, gram_b, merged, block,
    halo_s, halo_r, rs_s, rs_r, lat_s, lat_r, own_sem,
    c_s, c_r, d1_s, d1_r, d2_s, d2_r, e1_s, e1_r, e2_s, e2_r, f_s, f_r, loc_sem,
):
    m = lax.axis_index("image")
    band = lax.axis_index("band")
    depth, core = m // 2, m % 2
    y, x = band // 4, band % 4
    scale = 1152.0 ** -0.5

    barrier = pltpu.get_barrier_semaphore()

    @pl.loop(1, 16)
    def _(j):
        pl.semaphore_signal(
            barrier, inc=1, device_id={"image": m, "band": (band + j) % 16}, device_id_type=MESH
        )

    @pl.loop(1, 32)
    def _(j):
        pl.semaphore_signal(
            barrier, inc=1, device_id={"image": (m + j) % 32, "band": band}, device_id_type=MESH
        )

    for r in range(4):
        xbuf[:, 128 * (r + 1) : 128 * (r + 2)] = img[pl.ds(r, 128, stride=4), :]
        ybuf[:, 128 * (r + 1) : 128 * (r + 2)] = cot[pl.ds(r, 128, stride=4), :]
    pl.semaphore_wait(barrier, 46)

    def halo(buf, k, up):
        if up:
            return remote(
                buf.at[:, pl.ds(128, 128)], buf.at[:, pl.ds(640, 128)],
                halo_s.at[k], halo_r.at[k], m, band - 1,
            )
        return remote(
            buf.at[:, pl.ds(512, 128)], buf.at[:, pl.ds(0, 128)],
            halo_s.at[k], halo_r.at[k], m, band + 1,
        )

    @pl.when(band > 0)
    def _():
        halo(xbuf, 0, True).start()
        halo(ybuf, 2, True).start()

    @pl.when(band < 15)
    def _():
        halo(xbuf, 1, False).start()
        halo(ybuf, 3, False).start()

    for a in range(3):
        for b in range(3):
            w = fil[0, pl.ds(3 * a + b, 128, stride=9), :]
            hi, lo = halves(w.T)
            w1h[128 * b : 128 * b + 128, 128 * a : 128 * a + 128] = hi
            w1l[128 * b : 128 * b + 128, 128 * a : 128 * a + 128] = lo
            hi, lo = halves(fil[1, pl.ds(3 * a + b, 128, stride=9), :])
            w2h[128 * b : 128 * b + 128, 128 * a : 128 * a + 128] = hi
            w2l[128 * b : 128 * b + 128, 128 * a : 128 * a + 128] = lo

    @pl.when(band == 0)
    def _():
        xbuf[:, 0:128] = jnp.zeros((128, 128), F32)
        ybuf[:, 0:128] = jnp.zeros((128, 128), F32)

    @pl.when(band == 15)
    def _():
        xbuf[:, 640:768] = jnp.zeros((128, 128), F32)
        ybuf[:, 640:768] = jnp.zeros((128, 128), F32)

    @pl.when(band < 15)
    def _():
        halo(xbuf, 0, True).wait_recv()
        halo(ybuf, 2, True).wait_recv()

    @pl.when(band > 0)
    def _():
        halo(xbuf, 1, False).wait_recv()
        halo(ybuf, 3, False).wait_recv()

    for r in range(6):
        cols = slice(128 * r, 128 * r + 128)
        xh[:, cols], xl[:, cols] = halves(xbuf[:, cols])
        yh[:, cols], yl[:, cols] = halves(ybuf[:, cols])

    def stacked(ref, start, width, order):
        return jnp.concatenate([ref[:, 128 * a + start : 128 * a + start + width] for a in order], axis=0)

    def product(wh, wl, vh, vl, order):
        for half in range(2):
            hi = stacked(vh, 256 * half, 256, order)
            lo = stacked(vl, 256 * half, 256, order)
            z[:, 256 * half : 256 * half + 256] = nn(wh[...], hi) + (nn(wh[...], lo) + nn(wl[...], hi))

    product(w1h, w1l, xh, xl, (0, 1, 2))
    for r in range(4):
        cols = slice(128 * r, 128 * r + 128)
        pre = scale * (before(z[0:128, cols]) + z[128:256, cols] + after(z[256:384, cols]))
        sig = 1.0 / (1.0 + jnp.exp(-pre))
        hidden = scale * (pre * sig)
        dsig[:, cols] = (scale * scale) * (sig * (1.0 + pre * (1.0 - sig)))
        for b, v in enumerate((before(hidden), hidden, after(hidden))):
            hh[128 * b : 128 * b + 128, cols], hl[128 * b : 128 * b + 128, cols] = halves(v)

    for b in range(3):
        rows = slice(128 * b, 128 * b + 128)
        hi = stacked(yh, 0, 512, (2, 1, 0))
        lo = stacked(yl, 0, 512, (2, 1, 0))
        part = nt(hh[rows], hi) + (nt(hh[rows], lo) + nt(hl[rows], hi))
        ga[b] = part.reshape(4, 4, 8, 384)

    def ring_ids(axis, step):
        if axis == 0:
            return m, y * 4 + (x + step) % 4
        return m, ((y + step) % 4) * 4 + x

    def part_of(ref, axis, where, half):
        if axis == 0:
            return ref.at[:, pl.ds(2 * half, 2), where]
        return ref.at[:, where, pl.ds(2 * half, 2)]

    def ring_copies(g, opp, raw, summed, axis, base):
        at = x if axis == 0 else y
        right, left = ring_ids(axis, 1), ring_ids(axis, 3)
        far = (at + 2) % 4
        first = [
            remote(part_of(g, axis, far, 0), opp.at[0], rs_s.at[base], rs_r.at[base], *right),
            remote(part_of(g, axis, far, 1), opp.at[1], rs_s.at[base + 1], rs_r.at[base + 1], *left),
            remote(part_of(g, axis, (at + 1) % 4, 1), raw.at[1], rs_s.at[base + 2], rs_r.at[base + 2], *right),
            remote(part_of(g, axis, (at + 3) % 4, 0), raw.at[0], rs_s.at[base + 3], rs_r.at[base + 3], *left),
        ]
        second = [
            remote(opp.at[0], summed.at[0], rs_s.at[base + 4], rs_r.at[base + 4], *right),
            remote(opp.at[1], summed.at[1], rs_s.at[base + 5], rs_r.at[base + 5], *left),
        ]
        return first, second

    def ring_start(first):
        for c in first:
            c.start()

    def ring_pass(g, opp, first, second, axis):
        at = x if axis == 0 else y
        first[0].wait_recv()
        opp[0] += part_of(g, axis, (at + 1) % 4, 0)[...]
        second[0].start()
        first[1].wait_recv()
        opp[1] += part_of(g, axis, (at + 3) % 4, 1)[...]
        second[1].start()

    def ring_finish(g, raw, summed, stage, first, second, axis):
        at = x if axis == 0 else y
        first[2].wait_recv()
        first[3].wait_recv()
        second[0].wait_recv()
        second[1].wait_recv()
        for half in range(2):
            stage[:, pl.ds(2 * half, 2)] = part_of(g, axis, at, half)[...] + (raw[half] + summed[half])

    def last_copies(stage, landing, axis, base):
        at = x if axis == 0 else y
        return [
            remote(
                stage.at[:, (at + step) % 4], landing.at[step - 1],
                lat_s.at[base + step - 1], lat_r.at[base + step - 1], *ring_ids(axis, step),
            )
            for step in (1, 2, 3)
        ]

    ring_a = ring_copies(ga, oppa, rawa, suma, 0, 0)
    ring_start(ring_a[0])

    product(w2h, w2l, yh, yl, (2, 1, 0))
    for r in range(4):
        cols = slice(128 * r, 128 * r + 128)
        dhid = after(z[0:128, cols]) + z[128:256, cols] + before(z[256:384, cols])
        dpre = dhid * dsig[:, cols]
        for b, v in enumerate((after(dpre), dpre, before(dpre))):
            hh[128 * b : 128 * b + 128, cols], hl[128 * b : 128 * b + 128, cols] = halves(v)
    for a in range(3):
        hi, lo = xh[:, 128 * a : 128 * a + 512], xl[:, 128 * a : 128 * a + 512]
        part = nt(hi, hh[...]) + (nt(hi, hl[...]) + nt(lo, hh[...]))
        gb[a] = part.reshape(4, 4, 8, 384)

    ring_b = ring_copies(gb, oppb, rawb, sumb, 1, 6)
    ring_start(ring_b[0])
    ring_pass(ga, oppa, *ring_a, 0)
    ring_pass(gb, oppb, *ring_b, 1)
    ring_finish(ga, rawa, suma, stage_a, *ring_a, 0)
    last_a = last_copies(stage_a, lata, 1, 0)
    ring_start(last_a)
    ring_finish(gb, rawb, sumb, stage_b, *ring_b, 1)
    last_b = last_copies(stage_b, latb, 0, 3)
    ring_start(last_b)
    for c in last_a:
        c.wait_recv()
    sown[1] = stage_a[:, y] + (lata[0] + (lata[1] + lata[2]))
    for c in last_b:
        c.wait_recv()
    sown[0] = stage_b[:, x] + (latb[0] + (latb[1] + latb[2]))

    def tile_copy(layer, k):
        o, lane = k // 3, k % 3
        target = 2 * (k + 7 * layer) + layer
        return target, remote(
            sown.at[layer, o, :, pl.ds(128 * lane, 128)], tiles.at[m],
            c_s.at[9 * layer + k], c_r.at[0], target, band,
        )

    for layer in range(2):
        for k in range(9):
            target, copy = tile_copy(layer, k)

            @pl.when(target != m)
            def _():
                copy.start()

            @pl.when(target == m)
            def _():
                tiles[m] = sown[layer, k // 3, :, 128 * (k % 3) : 128 * (k % 3) + 128]

    mine = depth - 7 * core
    owner = (mine >= 0) & (mine < 9)
    first_owner = 7 * core

    @pl.when(owner)
    def _():
        pltpu.make_async_copy(tiles.at[pl.ds(0, 31)], tiles.at[pl.ds(0, 31)], c_r.at[0]).wait()
        flat = tiles.reshape(256, 128)
        total = jnp.zeros((32, 32), F32)
        for s in range(8):
            v = flat[pl.ds(s, 32, stride=8), :]
            total = total + lax.dot_general(
                v, v, (((1,), (1,)), ((), ())), preferred_element_type=F32, precision=HIGH
            )
        wide = jnp.concatenate([total[8 * q : 8 * q + 8] for q in range(4)], axis=1)
        gram_z[mine] = wide
        for step in range(1, 9):
            to = (mine + step) % 9
            remote(
                gram_z.at[mine], gram_z.at[mine], d1_s.at[step - 1], d1_r.at[0],
                2 * (first_owner + to) + core, band,
            ).start()
        pltpu.make_async_copy(gram_z.at[pl.ds(0, 8)], gram_z.at[pl.ds(0, 8)], d1_r.at[0]).wait()
        gram_b[band] = jnp.sum(gram_z[...], axis=0)

        @pl.loop(1, 16)
        def _(j):
            remote(
                gram_b.at[band], gram_b.at[band], d2_s.at[j - 1], d2_r.at[0], m, (band + j) % 16
            ).start()

        pltpu.make_async_copy(gram_b.at[pl.ds(0, 15)], gram_b.at[pl.ds(0, 15)], d2_r.at[0]).wait()
        packed = jnp.sum(gram_b[...], axis=0)
        rows = [packed if q == 0 else pltpu.roll(packed, 128 - 32 * q, 1) for q in range(4)]
        gram = jnp.concatenate(rows, axis=0)
        lane = lax.broadcasted_iota(jnp.int32, gram.shape, 1)
        alpha = adasum_weights(jnp.where(lane < 32, gram, 0.0))
        lines = [
            jnp.sum(flat[pl.ds(s, 32, stride=8), :] * alpha, axis=0, keepdims=True) for s in range(8)
        ]
        merged[mine] = jnp.concatenate(lines, axis=0)

        @pl.loop(1, 16)
        def _(j):
            remote(
                merged.at[mine], merged.at[mine], e1_s.at[j - 1], e1_r.at[0],
                2 * ((depth + j) % 16) + core, band,
            ).start()

        pltpu.make_async_copy(merged.at[pl.ds(0, 8)], merged.at[pl.ds(0, 8)], e1_r.at[0]).wait()

    @pl.when(jnp.logical_not(owner))
    def _():
        pltpu.make_async_copy(merged.at[pl.ds(0, 9)], merged.at[pl.ds(0, 9)], e1_r.at[0]).wait()

    def to_rows(layer):
        for k in range(9):
            t = k if layer == 0 else 3 * (k % 3) + k // 3
            block[pl.ds(t, 8, stride=9), :] = merged[k]
        start = pl.multiple_of(72 * band, 8)
        block[...] = fil[layer, pl.ds(start, 72), :] - rates[layer] * block[...]

    def spread(layer):
        start = pl.multiple_of(72 * band, 8)
        place = out.at[layer, pl.ds(start, 72)]
        sibling = 2 * depth + 1 - layer
        own = pltpu.make_async_copy(block, place, loc_sem.at[0])
        own.start()

        @pl.loop(1, 16)
        def _(j):
            remote(block, place, e2_s.at[j - 1], e2_r.at[j - 1], m, (band + j) % 16).start()

        pair = remote(block, place, f_s.at[0], f_r.at[0], sibling, band)
        pair.start()
        own.wait()

        @pl.loop(1, 16)
        def _(j):
            source = (band + 16 - j) % 16
            there = out.at[layer, pl.ds(pl.multiple_of(72 * source, 8), 72)]
            remote(block, there, e2_s.at[j - 1], e2_r.at[j - 1], m, band).wait_recv()
            remote(there, there, f_s.at[j], f_r.at[j], sibling, band).start()

        @pl.loop(0, 16)
        def _(j):
            source = (band + 16 - j) % 16
            there = out.at[1 - layer, pl.ds(pl.multiple_of(72 * source, 8), 72)]
            copy = remote(block, there, f_s.at[j], f_r.at[j], sibling, band)
            copy.wait_recv()
            copy.wait_send()

        @pl.loop(1, 16)
        def _(j):
            remote(block, place, e2_s.at[j - 1], e2_r.at[j - 1], m, band).wait_send()

    @pl.when(core == 0)
    def _():
        to_rows(0)
        spread(0)

    @pl.when(core == 1)
    def _():
        to_rows(1)
        spread(1)

    @pl.when(band > 0)
    def _():
        halo(xbuf, 0, True).wait_send()
        halo(ybuf, 2, True).wait_send()

    @pl.when(band < 15)
    def _():
        halo(xbuf, 1, False).wait_send()
        halo(ybuf, 3, False).wait_send()

    for c in (*ring_a[0], *ring_a[1], *ring_b[0], *ring_b[1], *last_a, *last_b):
        c.wait_send()
    for layer in range(2):
        for k in range(9):
            target, copy = tile_copy(layer, k)

            @pl.when(target != m)
            def _():
                copy.wait_send()

    @pl.when(owner)
    def _():
        for step in range(1, 9):
            remote(
                gram_z.at[mine], gram_z.at[mine], d1_s.at[step - 1], d1_r.at[0],
                2 * (first_owner + (mine + step) % 9) + core, band,
            ).wait_send()

        @pl.loop(1, 16)
        def _(j):
            remote(
                gram_b.at[band], gram_b.at[band], d2_s.at[j - 1], d2_r.at[0], m, (band + j) % 16
            ).wait_send()
            remote(
                merged.at[mine], merged.at[mine], e1_s.at[j - 1], e1_r.at[0],
                2 * ((depth + j) % 16) + core, band,
            ).wait_send()


def local(images, cotangent, filters, rates):
    vmem = pl.BlockSpec(memory_space=pltpu.VMEM)
    dma = pltpu.SemaphoreType.DMA
    new = pl.pallas_call(
        kernel,
        out_shape=jax.ShapeDtypeStruct((2, 1152, 128), F32),
        in_specs=[vmem, vmem, vmem, pl.BlockSpec(memory_space=pltpu.SMEM)],
        out_specs=pl.BlockSpec(memory_space=pl.ANY),
        scratch_shapes=[
            pltpu.VMEM((128, 768), F32),
            pltpu.VMEM((128, 768), F32),
            pltpu.VMEM((128, 768), BF16),
            pltpu.VMEM((128, 768), BF16),
            pltpu.VMEM((128, 768), BF16),
            pltpu.VMEM((128, 768), BF16),
            pltpu.VMEM((384, 384), BF16),
            pltpu.VMEM((384, 384), BF16),
            pltpu.VMEM((384, 384), BF16),
            pltpu.VMEM((384, 384), BF16),
            pltpu.VMEM((384, 512), F32),
            pltpu.VMEM((128, 512), F32),
            pltpu.VMEM((384, 512), BF16),
            pltpu.VMEM((384, 512), BF16),
            pltpu.VMEM((3, 4, 4, 8, 384), F32),
            pltpu.VMEM((3, 4, 4, 8, 384), F32),
            *[pltpu.VMEM((2, 3, 2, 8, 384), F32)] * 6,
            *[pltpu.VMEM((3, 4, 8, 384), F32)] * 2,
            *[pltpu.VMEM((3, 3, 8, 384), F32)] * 2,
            pltpu.VMEM((2, 3, 8, 384), F32),
            pltpu.VMEM((32, 8, 128), F32),
            pltpu.VMEM((9, 8, 128), F32),
            pltpu.VMEM((16, 8, 128), F32),
            pltpu.VMEM((9, 8, 128), F32),
            pltpu.VMEM((72, 128), F32),
            dma((4,)), dma((4,)), dma((12,)), dma((12,)), dma((6,)), dma((6,)), dma((1,)),
            dma((18,)), dma((1,)), dma((8,)), dma((1,)), dma((15,)), dma((1,)),
            dma((15,)), dma((1,)), dma((15,)), dma((15,)), dma((16,)), dma((16,)), dma((1,)),
        ],
        compiler_params=pltpu.CompilerParams(
            collective_id=0, has_side_effects=True, vmem_limit_bytes=48 * 1024 * 1024
        ),
        name="adasum_step",
    )(images.reshape(512, 128), cotangent.reshape(512, 128), filters, rates)
    return new[None]


def solution(mesh):
    return jax.shard_map(
        local,
        mesh=mesh,
        in_specs=(P("image", None, "band", None), P("image", None, "band", None), P(), P()),
        out_specs=P("image", None, None, None),
        check_vma=False,
    )
```

time: 213 us -> 83.8 us (0.39)
  the two profiles are of different devices: /device:TPU:2 before, /device:TPU:1 now
where the time goes in v1:
time: 83.8 us; the launch traced here: 83.6 us
  Pallas kernels  78.8 us (94%)
  local copies, waits for them, and re-layouts  4.84 us (6%)
    pallas_call x1, Pallas kernels, local(): pl.pallas_call(kernel, out_shape=jax.ShapeDtypeStruct((2, 1152, 128), F32...  78.8 us
    unnamed x9, local copies, waits for them, and re-layouts  4.84 us

profile of v1, /device:TPU:1, one launch (start us, length us, event | category | flops | bytes accessed | tf_op | source)
XLA Modules:
  0.0 83.6 jit_solution(13237531879950167621)
XLA Ops:
  0.0 0.0 copy-start
  0.0 1.3 %copy-done = f32[2,1152,128]{2,1,0:T(8,128)S(1)} copy-done((f32[2,1152,128]{2,1,0:T(8,128)S(1)}, f32[2,1152,128]{2,1,0:T(8,128)}, u32[]{:S(2)}) %copy-start) | copy-done | bytes 1179672
  1.3 0.0 copy-start.1
  1.3 0.9 %copy-done.1 = f32[1,128,4,128]{3,2,1,0:T(4,128)S(1)} copy-done((f32[1,128,4,128]{3,2,1,0:T(4,128)S(1)}, f32[1,128,4,128]{3,2,1,0:T(4,128)}, u32[]{:S(2)}) %copy-start.1) | copy-done | bytes 262168
  2.2 0.0 copy-start.2
  2.2 0.9 %copy-done.2 = f32[1,128,4,128]{3,2,1,0:T(4,128)S(1)} copy-done((f32[1,128,4,128]{3,2,1,0:T(4,128)S(1)}, f32[1,128,4,128]{3,2,1,0:T(4,128)}, u32[]{:S(2)}) %copy-start.2) | copy-done | bytes 262168
  3.2 0.0 copy-start.3
  3.2 0.7 copy-done.3
  3.8 78.8 %adasum_step.1 = f32[2,1152,128]{2,1,0:T(8,128)S(1)} custom-call(f32[512,128]{1,0:T(8,128)S(1)} %bitcast.4, f32[512,128]{1,0:T(8,128)S(1)} %bitcast.5, f32[2,1152,128]{2,1,0:T(8,128)S(1)} %copy-done, f32[2]{0:T(128)S(1)} %copy-done.3), custom_call_target="tpu_custom_call" | custom-call | tf_op jit(solution)/shard_map/adasum_step/pallas_call | solution.py:463
  82.6 1.0 %copy.6 = f32[1,2,1152,128]{3,2,1,0:T(8,128)} copy(f32[1,2,1152,128]{3,2,1,0:T(8,128)S(1)} %bitcast.3) | data formatting | bytes 2359296
Async XLA Ops:
  0.0 1.3 %copy-start = (f32[2,1152,128]{2,1,0:T(8,128)S(1)}, f32[2,1152,128]{2,1,0:T(8,128)}, u32[]{:S(2)}) copy-start(f32[2,1152,128]{2,1,0:T(8,128)} %fil.1) | copy-start | bytes 3538948
  1.3 0.9 %copy-start.1 = (f32[1,128,4,128]{3,2,1,0:T(4,128)S(1)}, f32[1,128,4,128]{3,2,1,0:T(4,128)}, u32[]{:S(2)}) copy-start(f32[1,128,4,128]{3,2,1,0:T(4,128)} %param.4) | copy-start | bytes 786436
  2.2 0.9 %copy-start.2 = (f32[1,128,4,128]{3,2,1,0:T(4,128)S(1)}, f32[1,128,4,128]{3,2,1,0:T(4,128)}, u32[]{:S(2)}) copy-start(f32[1,128,4,128]{3,2,1,0:T(4,128)} %param.5) | copy-start | bytes 786436
  3.2 0.7 copy-start.3

commit v2 on v1

v2 whole, which is shorter than its diff:
```python
import functools

import jax
import jax.numpy as jnp
from jax import lax
from jax.experimental import pallas as pl
from jax.experimental.pallas import tpu as pltpu
from jax.sharding import PartitionSpec as P

MESH = pl.DeviceIdType.MESH
F32 = jnp.float32
BF16 = jnp.bfloat16
HIGH = lax.Precision.HIGHEST


def remote(src, dst, send, recv, image, band):
    return pltpu.make_async_remote_copy(
        src_ref=src,
        dst_ref=dst,
        send_sem=send,
        recv_sem=recv,
        device_id={"image": image, "band": band},
        device_id_type=MESH,
    )


def halves(v):
    hi = v.astype(BF16)
    return hi, (v - hi.astype(F32)).astype(BF16)


def before(v):
    lane = lax.broadcasted_iota(jnp.int32, v.shape, 1)
    return jnp.where(lane == 0, 0.0, pltpu.roll(v, 1, 1))


def after(v):
    lane = lax.broadcasted_iota(jnp.int32, v.shape, 1)
    return jnp.where(lane == 127, 0.0, pltpu.roll(v, 127, 1))


def nn(a, b):
    return lax.dot_general(a, b, (((1,), (0,)), ((), ())), preferred_element_type=F32)


def nt(a, b):
    return lax.dot_general(a, b, (((1,), (1,)), ((), ())), preferred_element_type=F32)


def partner_sum(h, level):
    bit = 1 << level
    if bit >= 8:
        blocks = [h[8 * k : 8 * k + 8] for k in range(4)]
        other = jnp.concatenate([blocks[k ^ (bit // 8)] for k in range(4)], axis=0)
    else:
        blocks = []
        for k in range(4):
            v = h[8 * k : 8 * k + 8]
            r = lax.broadcasted_iota(jnp.int32, v.shape, 0)
            blocks.append(jnp.where((r & bit) == 0, pltpu.roll(v, 8 - bit, 0), pltpu.roll(v, bit, 0)))
        other = jnp.concatenate(blocks, axis=0)
    h = h + other
    lane = lax.broadcasted_iota(jnp.int32, h.shape, 1)
    other = jnp.where((lane & bit) == 0, pltpu.roll(h, 128 - bit, 1), pltpu.roll(h, bit, 1))
    return h + other


def adasum_weights(gram):
    row = lax.broadcasted_iota(jnp.int32, gram.shape, 0)
    lane = lax.broadcasted_iota(jnp.int32, gram.shape, 1)
    alpha = jnp.ones((32, 1), F32)
    for level in range(5):
        own = row == lane
        pair = row == (lane ^ (1 << level))
        sq = jnp.where(own, gram, 0.0)
        inner = jnp.where(pair, gram, 0.0)
        u_col = 1.0 - jnp.sum(inner, axis=1, keepdims=True) / (
            2.0 * (jnp.sum(sq, axis=1, keepdims=True) + 1e-6)
        )
        alpha = alpha * u_col
        if level < 4:
            u_row = 1.0 - jnp.sum(inner, axis=0, keepdims=True) / (
                2.0 * (jnp.sum(sq, axis=0, keepdims=True) + 1e-6)
            )
            gram = partner_sum(gram * u_col * u_row, level)
    return alpha


def thirds(v):
    hi = v.astype(BF16)
    v = v - hi.astype(F32)
    mid = v.astype(BF16)
    return hi, mid, (v - mid.astype(F32)).astype(BF16)


FAR_FIRST = (8, 7, 9, 6, 10, 5, 11, 4, 12, 3, 13, 2, 14, 1, 15)


def kernel(
    img_in, cot_in, fil_in, rates, out,
    img, cot, fil, xedge, yedge, xhalo, yhalo, xh, xl, yh, yl, w1h, w1l, w2h, w2l, z, hh, hl,
    ga, gb, oppa, oppb, rawa, rawb, suma, sumb, stage_a, stage_b, lata, latb, sown,
    held, gram_b, block,
    in_sem, halo_s, halo_r, rs_s, rs_r, lat_s, lat_r,
    c_s, c_r, d_s, d_r, e1_s, e1_r, e2_s, e2_r, f_s, f_r, loc_sem,
):
    m = lax.axis_index("image")
    band = lax.axis_index("band")
    depth, core = m // 2, m % 2
    y, x = band // 4, band % 4
    scale = 1152.0 ** -0.5

    barrier = pltpu.get_barrier_semaphore()

    @pl.loop(1, 16)
    def _(j):
        pl.semaphore_signal(
            barrier, inc=1, device_id={"image": m, "band": (band + j) % 16}, device_id_type=MESH
        )

    @pl.loop(1, 32)
    def _(j):
        pl.semaphore_signal(
            barrier, inc=1, device_id={"image": (m + j) % 32, "band": band}, device_id_type=MESH
        )

    loads = [
        pltpu.make_async_copy(src, dst, in_sem.at[k])
        for k, (src, dst) in enumerate(((img_in, img), (cot_in, cot), (fil_in, fil)))
    ]
    for c in loads:
        c.start()

    for c, field, edge, vh, vl in ((loads[0], img, xedge, xh, xl), (loads[1], cot, yedge, yh, yl)):
        c.wait()
        for r in range(4):
            v = field[pl.ds(r, 128, stride=4), :]
            if r % 3 == 0:
                edge[r // 3] = v
            cols = slice(128 * (r + 1), 128 * (r + 2))
            vh[:, cols], vl[:, cols] = halves(v)

    def halo(edge, landing, k, up):
        if up:
            return remote(edge.at[0], landing.at[1], halo_s.at[k], halo_r.at[k], m, band - 1)
        return remote(edge.at[1], landing.at[0], halo_s.at[k], halo_r.at[k], m, band + 1)

    loads[2].wait()
    for a in range(3):
        for b in range(3):
            rows, cols = slice(128 * b, 128 * b + 128), slice(128 * a, 128 * a + 128)
            w = fil[0, pl.ds(3 * a + b, 128, stride=9), :]
            w1h[rows, cols], w1l[rows, cols] = halves(w.T)
            w2h[rows, cols], w2l[rows, cols] = halves(fil[1, pl.ds(3 * a + b, 128, stride=9), :])

    def columns(ref, pair, offset):
        first, second = (128 * (r + offset) for r in pair)
        return jnp.concatenate([ref[:, first : first + 128], ref[:, second : second + 128]], axis=1)

    def stacked(ref, pair, order):
        return jnp.concatenate([columns(ref, pair, a) for a in order], axis=0)

    def product(wh, wl, hi, lo):
        z[...] = nn(wh[...], hi) + (nn(wh[...], lo) + nn(wl[...], hi))

    def hidden_of(pair):
        product(w1h, w1l, stacked(xh, pair, (0, 1, 2)), stacked(xl, pair, (0, 1, 2)))
        slopes = []
        for q in range(2):
            cols = slice(128 * q, 128 * q + 128)
            pre = scale * (before(z[0:128, cols]) + z[128:256, cols] + after(z[256:384, cols]))
            sig = 1.0 / (1.0 + jnp.exp(-pre))
            hidden = scale * (pre * sig)
            slopes.append((scale * scale) * (sig * (1.0 + pre * (1.0 - sig))))
            for b, v in enumerate((before(hidden), hidden, after(hidden))):
                hh[128 * b : 128 * b + 128, cols], hl[128 * b : 128 * b + 128, cols] = halves(v)
        return slopes

    def second_gradient(pair, add):
        hi, lo = stacked(yh, pair, (2, 1, 0)), stacked(yl, pair, (2, 1, 0))
        for b in range(3):
            rows = slice(128 * b, 128 * b + 128)
            part = nt(hh[rows], hi) + (nt(hh[rows], lo) + nt(hl[rows], hi))
            part = part.reshape(4, 4, 8, 384)
            ga[b] = ga[b] + part if add else part

    def first_gradient(pair, slopes, add):
        product(w2h, w2l, stacked(yh, pair, (2, 1, 0)), stacked(yl, pair, (2, 1, 0)))
        for q in range(2):
            cols = slice(128 * q, 128 * q + 128)
            dpre = (after(z[0:128, cols]) + z[128:256, cols] + before(z[256:384, cols])) * slopes[q]
            for b, v in enumerate((after(dpre), dpre, before(dpre))):
                hh[128 * b : 128 * b + 128, cols], hl[128 * b : 128 * b + 128, cols] = halves(v)
        for a in range(3):
            hi, lo = columns(xh, pair, a), columns(xl, pair, a)
            part = nt(hi, hh[...]) + (nt(hi, hl[...]) + nt(lo, hh[...]))
            part = part.reshape(4, 4, 8, 384)
            gb[a] = gb[a] + part if add else part

    slopes = hidden_of((1, 2))
    second_gradient((1, 2), False)
    first_gradient((1, 2), slopes, False)

    pl.semaphore_wait(barrier, 46)

    @pl.when(band > 0)
    def _():
        halo(xedge, xhalo, 0, True).start()
        halo(yedge, yhalo, 2, True).start()

    @pl.when(band < 15)
    def _():
        halo(xedge, xhalo, 1, False).start()
        halo(yedge, yhalo, 3, False).start()

    @pl.when(band == 0)
    def _():
        xhalo[0] = jnp.zeros((128, 128), F32)
        yhalo[0] = jnp.zeros((128, 128), F32)

    @pl.when(band == 15)
    def _():
        xhalo[1] = jnp.zeros((128, 128), F32)
        yhalo[1] = jnp.zeros((128, 128), F32)

    def halo_arrived(edge, landing, k):
        @pl.when(band < 15)
        def _():
            halo(edge, landing, k, True).wait_recv()

        @pl.when(band > 0)
        def _():
            halo(edge, landing, k + 1, False).wait_recv()

    halo_arrived(xedge, xhalo, 0)
    xh[:, 0:128], xl[:, 0:128] = halves(xhalo[0])
    xh[:, 640:768], xl[:, 640:768] = halves(xhalo[1])
    slopes = hidden_of((0, 3))
    halo_arrived(yedge, yhalo, 2)
    yh[:, 0:128], yl[:, 0:128] = halves(yhalo[0])
    yh[:, 640:768], yl[:, 640:768] = halves(yhalo[1])
    second_gradient((0, 3), True)

    def ring_ids(axis, step):
        if axis == 0:
            return m, y * 4 + (x + step) % 4
        return m, ((y + step) % 4) * 4 + x

    def part_of(ref, axis, where, half):
        if axis == 0:
            return ref.at[:, pl.ds(2 * half, 2), where]
        return ref.at[:, where, pl.ds(2 * half, 2)]

    def ring_copies(g, opp, raw, summed, axis, base):
        at = x if axis == 0 else y
        right, left = ring_ids(axis, 1), ring_ids(axis, 3)
        far = (at + 2) % 4
        first = [
            remote(part_of(g, axis, far, 0), opp.at[0], rs_s.at[base], rs_r.at[base], *right),
            remote(part_of(g, axis, far, 1), opp.at[1], rs_s.at[base + 1], rs_r.at[base + 1], *left),
            remote(part_of(g, axis, (at + 1) % 4, 1), raw.at[1], rs_s.at[base + 2], rs_r.at[base + 2], *right),
            remote(part_of(g, axis, (at + 3) % 4, 0), raw.at[0], rs_s.at[base + 3], rs_r.at[base + 3], *left),
        ]
        second = [
            remote(opp.at[0], summed.at[0], rs_s.at[base + 4], rs_r.at[base + 4], *right),
            remote(opp.at[1], summed.at[1], rs_s.at[base + 5], rs_r.at[base + 5], *left),
        ]
        return first, second

    def ring_start(first):
        for c in first:
            c.start()

    def ring_pass(g, opp, first, second, axis):
        at = x if axis == 0 else y
        first[0].wait_recv()
        opp[0] += part_of(g, axis, (at + 1) % 4, 0)[...]
        second[0].start()
        first[1].wait_recv()
        opp[1] += part_of(g, axis, (at + 3) % 4, 1)[...]
        second[1].start()

    def ring_finish(g, raw, summed, stage, first, second, axis):
        at = x if axis == 0 else y
        first[2].wait_recv()
        first[3].wait_recv()
        second[0].wait_recv()
        second[1].wait_recv()
        for half in range(2):
            stage[:, pl.ds(2 * half, 2)] = part_of(g, axis, at, half)[...] + (raw[half] + summed[half])

    def last_copies(stage, landing, axis, base):
        at = x if axis == 0 else y
        return [
            remote(
                stage.at[:, (at + step) % 4], landing.at[step - 1],
                lat_s.at[base + step - 1], lat_r.at[base + step - 1], *ring_ids(axis, step),
            )
            for step in (1, 2, 3)
        ]

    ring_a = ring_copies(ga, oppa, rawa, suma, 0, 0)
    ring_start(ring_a[0])

    first_gradient((0, 3), slopes, True)

    ring_b = ring_copies(gb, oppb, rawb, sumb, 1, 6)
    ring_start(ring_b[0])
    ring_pass(ga, oppa, *ring_a, 0)
    ring_pass(gb, oppb, *ring_b, 1)
    ring_finish(ga, rawa, suma, stage_a, *ring_a, 0)
    last_a = last_copies(stage_a, lata, 1, 0)
    ring_start(last_a)
    ring_finish(gb, rawb, sumb, stage_b, *ring_b, 1)
    last_b = last_copies(stage_b, latb, 0, 3)
    ring_start(last_b)

    owners = (0, 17)

    def to_owner(layer):
        return remote(sown.at[layer], held.at[m], c_s.at[layer], c_r.at[0], owners[layer], band)

    def hand_over(layer):
        @pl.when(m != owners[layer])
        def _():
            to_owner(layer).start()

        @pl.when(m == owners[layer])
        def _():
            held[m] = sown[layer]

    def keep(layer, total):
        for k in range(9):
            sown[layer, k] = total[k // 3, :, 128 * (k % 3) : 128 * (k % 3) + 128]

    for c in last_a:
        c.wait_recv()
    keep(1, stage_a[:, y] + (lata[0] + (lata[1] + lata[2])))
    hand_over(1)
    for c in last_b:
        c.wait_recv()
    keep(0, stage_b[:, x] + (latb[0] + (latb[1] + latb[2])))
    hand_over(0)

    owner = (m == owners[0]) | (m == owners[1])

    def gram_copy(j):
        return remote(gram_b.at[band], gram_b.at[band], d_s.at[j - 1], d_r.at[0], m, (band + j) % 16)

    def block_copy(k):
        return remote(block, block, e1_s.at[k], e1_r.at[0], 2 * ((depth + FAR_FIRST[k]) % 16) + core, band)

    def finish(layer, alpha):
        totals = [alpha[0:1] * held[0, k] for k in range(9)]
        for q in range(1, 32):
            totals = [v + alpha[q : q + 1] * held[q, k] for k, v in enumerate(totals)]
        for k, v in enumerate(totals):
            t = k if layer == 0 else 3 * (k % 3) + k // 3
            block[pl.ds(t, 8, stride=9), :] = v
        start = pl.multiple_of(72 * band, 8)
        block[...] = fil[layer, pl.ds(start, 72), :] - rates[layer] * block[...]

    @pl.when(owner)
    def _():
        pltpu.make_async_copy(held.at[pl.ds(0, 31)], held.at[pl.ds(0, 31)], c_r.at[0]).wait()
        flat = held.reshape(2304, 128)
        total = jnp.zeros((96, 96), F32)
        for row in range(0, 72, 4):
            lines = [flat[pl.ds(row + q, 32, stride=72), :] for q in range(4)]
            v = jnp.concatenate(thirds(jnp.concatenate(lines, axis=1)), axis=0)
            total = total + nt(v, v)
        total = total[0:32] + total[32:64] + total[64:96]
        total = total[:, 0:32] + total[:, 32:64] + total[:, 64:96]
        gram_b[band] = jnp.concatenate([total[8 * q : 8 * q + 8] for q in range(4)], axis=1)

        @pl.loop(1, 16)
        def _(j):
            gram_copy(j).start()

        pltpu.make_async_copy(gram_b.at[pl.ds(0, 15)], gram_b.at[pl.ds(0, 15)], d_r.at[0]).wait()
        packed = jnp.sum(gram_b[...], axis=0)
        rows = [packed if q == 0 else pltpu.roll(packed, 128 - 32 * q, 1) for q in range(4)]
        gram = jnp.concatenate(rows, axis=0)
        lane = lax.broadcasted_iota(jnp.int32, gram.shape, 1)
        alpha = adasum_weights(jnp.where(lane < 32, gram, 0.0))
        for layer in range(2):
            @pl.when(core == layer)
            def _():
                finish(layer, alpha)

        for k in range(15):
            block_copy(k).start()

    @pl.when(jnp.logical_not(owner))
    def _():
        pltpu.make_async_copy(block, block, e1_r.at[0]).wait()

    start = pl.multiple_of(72 * band, 8)
    place = out.at[core, pl.ds(start, 72)]
    sibling = 2 * depth + 1 - core
    own = pltpu.make_async_copy(block, place, loc_sem.at[0])
    own.start()

    @pl.loop(1, 16)
    def _(j):
        remote(block, place, e2_s.at[j - 1], e2_r.at[j - 1], m, (band + j) % 16).start()

    remote(block, place, f_s.at[0], f_r.at[0], sibling, band).start()

    @pl.loop(1, 16)
    def _(j):
        source = (band + 16 - j) % 16
        there = out.at[core, pl.ds(pl.multiple_of(72 * source, 8), 72)]
        remote(block, there, e2_s.at[j - 1], e2_r.at[j - 1], m, band).wait_recv()
        remote(there, there, f_s.at[j], f_r.at[j], sibling, band).start()

    @pl.loop(0, 16)
    def _(j):
        source = (band + 16 - j) % 16
        there = out.at[1 - core, pl.ds(pl.multiple_of(72 * source, 8), 72)]
        copy = remote(block, there, f_s.at[j], f_r.at[j], sibling, band)
        copy.wait_recv()
        copy.wait_send()

    own.wait()

    @pl.loop(1, 16)
    def _(j):
        remote(block, place, e2_s.at[j - 1], e2_r.at[j - 1], m, band).wait_send()

    @pl.when(band > 0)
    def _():
        halo(xedge, xhalo, 0, True).wait_send()
        halo(yedge, yhalo, 2, True).wait_send()

    @pl.when(band < 15)
    def _():
        halo(xedge, xhalo, 1, False).wait_send()
        halo(yedge, yhalo, 3, False).wait_send()

    for c in (*ring_a[0], *ring_a[1], *ring_b[0], *ring_b[1], *last_a, *last_b):
        c.wait_send()
    for layer in range(2):
        @pl.when(m != owners[layer])
        def _():
            to_owner(layer).wait_send()

    @pl.when(owner)
    def _():
        for k in range(15):
            block_copy(k).wait_send()

        @pl.loop(1, 16)
        def _(j):
            gram_copy(j).wait_send()


def local(images, cotangent, filters, rates):
    dma = pltpu.SemaphoreType.DMA
    hbm = pl.BlockSpec(memory_space=pltpu.HBM)
    vmem = pltpu.VMEM
    new = pl.pallas_call(
        kernel,
        out_shape=jax.ShapeDtypeStruct((2, 1152, 128), F32),
        in_specs=[hbm, hbm, hbm, pl.BlockSpec(memory_space=pltpu.SMEM)],
        out_specs=hbm,
        scratch_shapes=[
            vmem((512, 128), F32), vmem((512, 128), F32), vmem((2, 1152, 128), F32),
            *[vmem((2, 128, 128), F32)] * 4,
            *[vmem((128, 768), BF16)] * 4,
            *[vmem((384, 384), BF16)] * 4,
            vmem((384, 256), F32),
            *[vmem((384, 256), BF16)] * 2,
            *[vmem((3, 4, 4, 8, 384), F32)] * 2,
            *[vmem((2, 3, 2, 8, 384), F32)] * 6,
            *[vmem((3, 4, 8, 384), F32)] * 2,
            *[vmem((3, 3, 8, 384), F32)] * 2,
            vmem((2, 9, 8, 128), F32),
            vmem((32, 9, 8, 128), F32),
            vmem((16, 8, 128), F32),
            vmem((72, 128), F32),
            dma((3,)), dma((4,)), dma((4,)), dma((12,)), dma((12,)), dma((6,)), dma((6,)),
            dma((2,)), dma((1,)), dma((15,)), dma((1,)), dma((15,)), dma((1,)),
            dma((15,)), dma((15,)), dma((16,)), dma((16,)), dma((1,)),
        ],
        compiler_params=pltpu.CompilerParams(
            collective_id=0, has_side_effects=True, vmem_limit_bytes=61 * 1024 * 1024
        ),
        name="adasum_step",
    )(images.reshape(512, 128), cotangent.reshape(512, 128), filters, rates)
    return new[None]


def solution(mesh):
    return jax.shard_map(
        local,
        mesh=mesh,
        in_specs=(P("image", None, "band", None), P("image", None, "band", None), P(), P()),
        out_specs=P("image", None, None, None),
        check_vma=False,
    )
```

time: 83.8 us -> 69.8 us (0.83)
  the two profiles are of different devices: /device:TPU:1 before, /device:TPU:33 now
where the time goes in v2:
time: 69.8 us; the launch traced here: 69.6 us
  Pallas kernels  67.2 us (96%)
  local copies, waits for them, and re-layouts  2.36 us (3%)
    pallas_call x1, Pallas kernels, local(): pl.pallas_call(kernel, out_shape=jax.ShapeDtypeStruct((2, 1152, 128), F32...  67.2 us
    unnamed x1, local copies, waits for them, and re-layouts  2.36 us

profile of v2, /device:TPU:33, one launch (start us, length us, event | category | flops | bytes accessed | tf_op | source)
XLA Modules:
  0.0 69.6 jit_solution(11960760522028047150)
XLA Ops:
  0.0 67.2 %adasum_step.1 = f32[2,1152,128]{2,1,0:T(8,128)} custom-call(f32[512,128]{1,0:T(8,128)} %bitcast.4, f32[512,128]{1,0:T(8,128)} %bitcast.5, f32[2,1152,128]{2,1,0:T(8,128)} %fil_in.1, f32[2]{0:T(128)} %rates.1), custom_call_target="tpu_custom_call" | custom-call | tf_op jit(solution)/shard_map/adasum_step/pallas_call | solution.py:462
  67.3 2.4 %copy.6 = f32[1,2,1152,128]{3,2,1,0:T(8,128)} copy(f32[1,2,1152,128]{3,2,1,0:T(8,128)} %bitcast.3) | data formatting | bytes 2359296

commit v3 on v2

--- a/solution.py
+++ b/solution.py
@@ -97,11 +97,11 @@
 
 
 def kernel(
-    img_in, cot_in, fil_in, rates, out,
+    img_in, cot_in, fil_in, out,
     img, cot, fil, xedge, yedge, xhalo, yhalo, xh, xl, yh, yl, w1h, w1l, w2h, w2l, z, hh, hl,
-    ga, gb, oppa, oppb, rawa, rawb, suma, sumb, stage_a, stage_b, lata, latb, sown,
+    ga, gb, along_x, along_y, sum_x, sum_y, landed, sown,
     held, gram_b, block,
-    in_sem, halo_s, halo_r, rs_s, rs_r, lat_s, lat_r,
+    in_sem, halo_s, halo_r, rs_s, rs_r, last_s, last_r,
     c_s, c_r, d_s, d_r, e1_s, e1_r, e2_s, e2_r, f_s, f_r, loc_sem,
 ):
     m = lax.axis_index("image")
@@ -112,17 +112,18 @@
 
     barrier = pltpu.get_barrier_semaphore()
 
+    def tell(sem, image, place):
+        pl.semaphore_signal(
+            sem, inc=1, device_id={"image": image, "band": place}, device_id_type=MESH
+        )
+
     @pl.loop(1, 16)
     def _(j):
-        pl.semaphore_signal(
-            barrier, inc=1, device_id={"image": m, "band": (band + j) % 16}, device_id_type=MESH
-        )
+        tell(barrier, m, (band + j) % 16)
 
     @pl.loop(1, 32)
     def _(j):
-        pl.semaphore_signal(
-            barrier, inc=1, device_id={"image": (m + j) % 32, "band": band}, device_id_type=MESH
-        )
+        tell(barrier, (m + j) % 32, band)
 
     loads = [
         pltpu.make_async_copy(src, dst, in_sem.at[k])
@@ -181,7 +182,7 @@
         for b in range(3):
             rows = slice(128 * b, 128 * b + 128)
             part = nt(hh[rows], hi) + (nt(hh[rows], lo) + nt(hl[rows], hi))
-            part = part.reshape(4, 4, 8, 384)
+            part = part.reshape(2, 2, 2, 2, 8, 384)
             ga[b] = ga[b] + part if add else part
 
     def first_gradient(pair, slopes, add):
@@ -194,7 +195,7 @@
         for a in range(3):
             hi, lo = columns(xh, pair, a), columns(xl, pair, a)
             part = nt(hi, hh[...]) + (nt(hi, hl[...]) + nt(lo, hh[...]))
-            part = part.reshape(4, 4, 8, 384)
+            part = part.reshape(2, 2, 2, 2, 8, 384)
             gb[a] = gb[a] + part if add else part
 
     slopes = hidden_of((1, 2))
@@ -206,11 +207,17 @@
     @pl.when(band > 0)
     def _():
         halo(xedge, xhalo, 0, True).start()
+
+    @pl.when(band < 15)
+    def _():
+        halo(xedge, xhalo, 1, False).start()
+
+    @pl.when(band > 0)
+    def _():
         halo(yedge, yhalo, 2, True).start()
 
     @pl.when(band < 15)
     def _():
-        halo(xedge, xhalo, 1, False).start()
         halo(yedge, yhalo, 3, False).start()
 
     @pl.when(band == 0)
@@ -241,79 +248,78 @@
     yh[:, 640:768], yl[:, 640:768] = halves(yhalo[1])
     second_gradient((0, 3), True)
 
-    def ring_ids(axis, step):
-        if axis == 0:
-            return m, y * 4 + (x + step) % 4
-        return m, ((y + step) % 4) * 4 + x
-
-    def part_of(ref, axis, where, half):
-        if axis == 0:
-            return ref.at[:, pl.ds(2 * half, 2), where]
-        return ref.at[:, where, pl.ds(2 * half, 2)]
-
-    def ring_copies(g, opp, raw, summed, axis, base):
-        at = x if axis == 0 else y
-        right, left = ring_ids(axis, 1), ring_ids(axis, 3)
-        far = (at + 2) % 4
-        first = [
-            remote(part_of(g, axis, far, 0), opp.at[0], rs_s.at[base], rs_r.at[base], *right),
-            remote(part_of(g, axis, far, 1), opp.at[1], rs_s.at[base + 1], rs_r.at[base + 1], *left),
-            remote(part_of(g, axis, (at + 1) % 4, 1), raw.at[1], rs_s.at[base + 2], rs_r.at[base + 2], *right),
-            remote(part_of(g, axis, (at + 3) % 4, 0), raw.at[0], rs_s.at[base + 3], rs_r.at[base + 3], *left),
-        ]
-        second = [
-            remote(opp.at[0], summed.at[0], rs_s.at[base + 4], rs_r.at[base + 4], *right),
-            remote(opp.at[1], summed.at[1], rs_s.at[base + 5], rs_r.at[base + 5], *left),
-        ]
-        return first, second
-
-    def ring_start(first):
-        for c in first:
-            c.start()
-
-    def ring_pass(g, opp, first, second, axis):
-        at = x if axis == 0 else y
-        first[0].wait_recv()
-        opp[0] += part_of(g, axis, (at + 1) % 4, 0)[...]
-        second[0].start()
-        first[1].wait_recv()
-        opp[1] += part_of(g, axis, (at + 3) % 4, 1)[...]
-        second[1].start()
-
-    def ring_finish(g, raw, summed, stage, first, second, axis):
-        at = x if axis == 0 else y
-        first[2].wait_recv()
-        first[3].wait_recv()
-        second[0].wait_recv()
-        second[1].wait_recv()
+    x_half, x_odd, y_half, y_odd = x // 2, x % 2, y // 2, y % 2
+
+    def first_copies(layer, g):
+        copies = []
+        for step in (1, 2, 3):
+            to = (x + step) % 4
+            k = 6 * layer + step - 1
+            copies.append(
+                remote(
+                    g.at[:, :, to % 2, to // 2, to % 2], along_x.at[layer, step - 1],
+                    rs_s.at[k], rs_r.at[k], m, y * 4 + to,
+                )
+            )
+            to = (y + step) % 4
+            copies.append(
+                remote(
+                    g.at[:, to // 2, to % 2, :, 1 - to % 2], along_y.at[layer, step - 1],
+                    rs_s.at[k + 3], rs_r.at[k + 3], m, to * 4 + x,
+                )
+            )
+        return copies
+
+    def last_copies(layer):
+        copies = []
         for half in range(2):
-            stage[:, pl.ds(2 * half, 2)] = part_of(g, axis, at, half)[...] + (raw[half] + summed[half])
-
-    def last_copies(stage, landing, axis, base):
-        at = x if axis == 0 else y
-        return [
+            to = 2 * half + x_odd
+            slot = (y - to + 3) % 4
+            copies.append((to != y, remote(
+                sum_x.at[layer, :, half], landed.at[layer, slot],
+                last_s.at[4 * layer + half], last_r.at[3 * layer + slot], m, to * 4 + x,
+            )))
+            to = 2 * half + 1 - y_odd
+            slot = (x - to + 3) % 4
+            copies.append((to != x, remote(
+                sum_y.at[layer, :, half], landed.at[layer, slot],
+                last_s.at[4 * layer + 2 + half], last_r.at[3 * layer + slot], m, y * 4 + to,
+            )))
+        return copies
+
+    def pass_on(layer, g):
+        for c in first_copies(layer, g):
+            c.wait_recv()
+        sum_x[layer] = g[:, :, x_odd, x_half, x_odd] + (
+            along_x[layer, 0] + (along_x[layer, 1] + along_x[layer, 2])
+        )
+        sum_y[layer] = g[:, y_half, y_odd, :, 1 - y_odd] + (
+            along_y[layer, 0] + (along_y[layer, 1] + along_y[layer, 2])
+        )
+        for going, c in last_copies(layer):
+            @pl.when(going)
+            def _():
+                c.start()
+
+    def take(layer):
+        for slot in range(3):
             remote(
-                stage.at[:, (at + step) % 4], landing.at[step - 1],
-                lat_s.at[base + step - 1], lat_r.at[base + step - 1], *ring_ids(axis, step),
-            )
-            for step in (1, 2, 3)
-        ]
-
-    ring_a = ring_copies(ga, oppa, rawa, suma, 0, 0)
-    ring_start(ring_a[0])
-
+                landed.at[layer, slot], landed.at[layer, slot],
+                last_s.at[0], last_r.at[3 * layer + slot], m, band,
+            ).wait_recv()
+        own = jnp.where(x_odd == y_odd, sum_x[layer, :, y_half], sum_y[layer, :, x_half])
+        total = own + (landed[layer, 0] + (landed[layer, 1] + landed[layer, 2]))
+        for k in range(9):
+            sown[layer, k] = total[k // 3, :, 128 * (k % 3) : 128 * (k % 3) + 128]
+
+    for c in first_copies(1, ga):
+        c.start()
     first_gradient((0, 3), slopes, True)
 
-    ring_b = ring_copies(gb, oppb, rawb, sumb, 1, 6)
-    ring_start(ring_b[0])
-    ring_pass(ga, oppa, *ring_a, 0)
-    ring_pass(gb, oppb, *ring_b, 1)
-    ring_finish(ga, rawa, suma, stage_a, *ring_a, 0)
-    last_a = last_copies(stage_a, lata, 1, 0)
-    ring_start(last_a)
-    ring_finish(gb, rawb, sumb, stage_b, *ring_b, 1)
-    last_b = last_copies(stage_b, latb, 0, 3)
-    ring_start(last_b)
+    for c in first_copies(0, gb):
+        c.start()
+    pass_on(1, ga)
+    pass_on(0, gb)
 
     owners = (0, 17)
 
@@ -329,17 +335,9 @@
         def _():
             held[m] = sown[layer]
 
-    def keep(layer, total):
-        for k in range(9):
-            sown[layer, k] = total[k // 3, :, 128 * (k % 3) : 128 * (k % 3) + 128]
-
-    for c in last_a:
-        c.wait_recv()
-    keep(1, stage_a[:, y] + (lata[0] + (lata[1] + lata[2])))
+    take(1)
     hand_over(1)
-    for c in last_b:
-        c.wait_recv()
-    keep(0, stage_b[:, x] + (latb[0] + (latb[1] + latb[2])))
+    take(0)
     hand_over(0)
 
     owner = (m == owners[0]) | (m == owners[1])
@@ -357,8 +355,6 @@
         for k, v in enumerate(totals):
             t = k if layer == 0 else 3 * (k % 3) + k // 3
             block[pl.ds(t, 8, stride=9), :] = v
-        start = pl.multiple_of(72 * band, 8)
-        block[...] = fil[layer, pl.ds(start, 72), :] - rates[layer] * block[...]
 
     @pl.when(owner)
     def _():
@@ -438,8 +434,13 @@
         halo(xedge, xhalo, 1, False).wait_send()
         halo(yedge, yhalo, 3, False).wait_send()
 
-    for c in (*ring_a[0], *ring_a[1], *ring_b[0], *ring_b[1], *last_a, *last_b):
-        c.wait_send()
+    for layer, g in ((0, gb), (1, ga)):
+        for c in first_copies(layer, g):
+            c.wait_send()
+        for going, c in last_copies(layer):
+            @pl.when(going)
+            def _():
+                c.wait_send()
     for layer in range(2):
         @pl.when(m != owners[layer])
         def _():
@@ -459,10 +460,10 @@
     dma = pltpu.SemaphoreType.DMA
     hbm = pl.BlockSpec(memory_space=pltpu.HBM)
     vmem = pltpu.VMEM
-    new = pl.pallas_call(
+    merged = pl.pallas_call(
         kernel,
         out_shape=jax.ShapeDtypeStruct((2, 1152, 128), F32),
-        in_specs=[hbm, hbm, hbm, pl.BlockSpec(memory_space=pltpu.SMEM)],
+        in_specs=[hbm, hbm, hbm],
         out_specs=hbm,
         scratch_shapes=[
             vmem((512, 128), F32), vmem((512, 128), F32), vmem((2, 1152, 128), F32),
@@ -471,15 +472,16 @@
             *[vmem((384, 384), BF16)] * 4,
             vmem((384, 256), F32),
             *[vmem((384, 256), BF16)] * 2,
-            *[vmem((3, 4, 4, 8, 384), F32)] * 2,
-            *[vmem((2, 3, 2, 8, 384), F32)] * 6,
-            *[vmem((3, 4, 8, 384), F32)] * 2,
-            *[vmem((3, 3, 8, 384), F32)] * 2,
+            *[vmem((3, 2, 2, 2, 2, 8, 384), F32)] * 2,
+            *[vmem((2, 3, 3, 2, 8, 384), F32)] * 2,
+            *[vmem((2, 3, 2, 8, 384), F32)] * 2,
+            vmem((2, 3, 3, 8, 384), F32),
             vmem((2, 9, 8, 128), F32),
             vmem((32, 9, 8, 128), F32),
             vmem((16, 8, 128), F32),
             vmem((72, 128), F32),
-            dma((3,)), dma((4,)), dma((4,)), dma((12,)), dma((12,)), dma((6,)), dma((6,)),
+            dma((3,)), dma((4,)), dma((4,)),
+            dma((12,)), dma((12,)), dma((8,)), dma((6,)),
             dma((2,)), dma((1,)), dma((15,)), dma((1,)), dma((15,)), dma((1,)),
             dma((15,)), dma((15,)), dma((16,)), dma((16,)), dma((1,)),
         ],
@@ -487,8 +489,8 @@
             collective_id=0, has_side_effects=True, vmem_limit_bytes=61 * 1024 * 1024
         ),
         name="adasum_step",
-    )(images.reshape(512, 128), cotangent.reshape(512, 128), filters, rates)
-    return new[None]
+    )(images.reshape(512, 128), cotangent.reshape(512, 128), filters)
+    return (filters - rates[:, None, None] * merged)[None]
 
 
 def solution(mesh):

time: 69.8 us -> 68.3 us (0.979)
  other arithmetic: 0 us -> 2.46 us
  local copies, waits for them, and re-layouts: 2.36 us -> 0.01 us
  Pallas kernels: 67.2 us -> 65.6 us
    broadcast_in_dim x0 -> x1, other arithmetic: none -> 2.46 us  [local(): return (filters - rates[:, None, None] * merged)[None]]
    unnamed x1 -> x4, local copies, waits for them, and re-layouts: 2.36 us -> 0.01 us
    pallas_call x1, Pallas kernels: 67.2 us -> 65.6 us  [local(): pl.pallas_call(kernel, out_shape=jax.ShapeDtypeStruct((2, 1152, 128), F32...]
where the time goes in v3:
time: 68.3 us; the launch traced here: 68.1 us
  Pallas kernels  65.6 us (96%)
  other arithmetic  2.46 us (4%)
    pallas_call x1, Pallas kernels, local(): pl.pallas_call(kernel, out_shape=jax.ShapeDtypeStruct((2, 1152, 128), F32...  65.6 us
    broadcast_in_dim x1, other arithmetic, local(): return (filters - rates[:, None, None] * merged)[None]  2.46 us

profile of v3, /device:TPU:33, one launch (start us, length us, event | category | flops | bytes accessed | tf_op | source)
XLA Modules:
  0.0 68.1 jit_solution(17615184056340022604)
XLA Ops:
  0.0 0.0 copy-start
  0.0 0.0 copy-start.1
  0.0 65.6 %adasum_step.1 = f32[2,1152,128]{2,1,0:T(8,128)} custom-call(f32[512,128]{1,0:T(8,128)} %bitcast.4, f32[512,128]{1,0:T(8,128)} %bitcast.5, f32[2,1152,128]{2,1,0:T(8,128)} %fil_in.1), custom_call_target="tpu_custom_call" | custom-call | tf_op jit(solution)/shard_map/adasum_step/pallas_call | solution.py:463
  65.6 0.0 copy-done
  65.6 0.0 copy-done.1
  65.6 2.5 %subtract_bitcast_fusion = f32[1,2,1152,128]{3,2,1,0:T(8,128)} fusion(f32[2,1152,128]{2,1,0:T(8,128)S(1)} %copy-done, f32[2,1152,128]{2,1,0:T(8,128)} %adasum_step.1, f32[2]{0:T(128)S(1)} %copy-done.1), kind=kLoop, calls=%fused_computation | loop fusion | flops 589824 | bytes 3538952 | tf_op jit(solution)/shard_map/broadcast_in_dim | solution.py:493
Async XLA Ops:
  0.0 65.6 %copy-start = (f32[2,1152,128]{2,1,0:T(8,128)S(1)}, f32[2,1152,128]{2,1,0:T(8,128)}, u32[]{:S(2)}) copy-start(f32[2,1152,128]{2,1,0:T(8,128)} %fil_in.1) | copy-start | bytes 3538948
  0.0 65.6 %copy-start.1 = (f32[2]{0:T(128)S(1)}, f32[2]{0:T(128)}, u32[]{:S(2)}) copy-start(f32[2]{0:T(128)} %param.7) | copy-start | bytes 28

commit v4 on v3

--- a/solution.py
+++ b/solution.py
@@ -93,7 +93,8 @@
     return hi, mid, (v - mid.astype(F32)).astype(BF16)
 
 
-FAR_FIRST = (8, 7, 9, 6, 10, 5, 11, 4, 12, 3, 13, 2, 14, 1, 15)
+OWNERS = (2, 9)
+ORDER = (0, 1, 2, 3, 4, 15, 5, 14, 6, 13, 7, 12, 8, 11, 9, 10)
 
 
 def kernel(
@@ -117,13 +118,23 @@
             sem, inc=1, device_id={"image": image, "band": place}, device_id_type=MESH
         )
 
+    sibling = m + 1 - 2 * core
+    owner = (m == OWNERS[0]) | (m == OWNERS[1])
+    beside_owner = (sibling == OWNERS[0]) | (sibling == OWNERS[1])
+
     @pl.loop(1, 16)
     def _(j):
         tell(barrier, m, (band + j) % 16)
 
-    @pl.loop(1, 32)
-    def _(j):
-        tell(barrier, (m + j) % 32, band)
+    @pl.when(owner)
+    def _():
+        @pl.loop(1, 32)
+        def _(j):
+            tell(barrier, (m + j) % 32, band)
+
+    @pl.when(jnp.logical_not(owner))
+    def _():
+        tell(barrier, sibling, band)
 
     loads = [
         pltpu.make_async_copy(src, dst, in_sem.at[k])
@@ -145,6 +156,31 @@
         if up:
             return remote(edge.at[0], landing.at[1], halo_s.at[k], halo_r.at[k], m, band - 1)
         return remote(edge.at[1], landing.at[0], halo_s.at[k], halo_r.at[k], m, band + 1)
+
+    @pl.when(owner | beside_owner)
+    def _():
+        pl.semaphore_wait(barrier, 17)
+
+    @pl.when(jnp.logical_not(owner | beside_owner))
+    def _():
+        pl.semaphore_wait(barrier, 18)
+
+
+    @pl.when(band > 0)
+    def _():
+        halo(xedge, xhalo, 0, True).start()
+
+    @pl.when(band < 15)
+    def _():
+        halo(xedge, xhalo, 1, False).start()
+
+    @pl.when(band > 0)
+    def _():
+        halo(yedge, yhalo, 2, True).start()
+
+    @pl.when(band < 15)
+    def _():
+        halo(yedge, yhalo, 3, False).start()
 
     loads[2].wait()
     for a in range(3):
@@ -201,24 +237,6 @@
     slopes = hidden_of((1, 2))
     second_gradient((1, 2), False)
     first_gradient((1, 2), slopes, False)
-
-    pl.semaphore_wait(barrier, 46)
-
-    @pl.when(band > 0)
-    def _():
-        halo(xedge, xhalo, 0, True).start()
-
-    @pl.when(band < 15)
-    def _():
-        halo(xedge, xhalo, 1, False).start()
-
-    @pl.when(band > 0)
-    def _():
-        halo(yedge, yhalo, 2, True).start()
-
-    @pl.when(band < 15)
-    def _():
-        halo(yedge, yhalo, 3, False).start()
 
     @pl.when(band == 0)
     def _():
@@ -321,17 +339,15 @@
     pass_on(1, ga)
     pass_on(0, gb)
 
-    owners = (0, 17)
-
     def to_owner(layer):
-        return remote(sown.at[layer], held.at[m], c_s.at[layer], c_r.at[0], owners[layer], band)
+        return remote(sown.at[layer], held.at[m], c_s.at[layer], c_r.at[0], OWNERS[layer], band)
 
     def hand_over(layer):
-        @pl.when(m != owners[layer])
+        @pl.when(m != OWNERS[layer])
         def _():
             to_owner(layer).start()
 
-        @pl.when(m == owners[layer])
+        @pl.when(m == OWNERS[layer])
         def _():
             held[m] = sown[layer]
 
@@ -340,13 +356,11 @@
     take(0)
     hand_over(0)
 
-    owner = (m == owners[0]) | (m == owners[1])
-
     def gram_copy(j):
         return remote(gram_b.at[band], gram_b.at[band], d_s.at[j - 1], d_r.at[0], m, (band + j) % 16)
 
-    def block_copy(k):
-        return remote(block, block, e1_s.at[k], e1_r.at[0], 2 * ((depth + FAR_FIRST[k]) % 16) + core, band)
+    def block_copy(to):
+        return remote(block, block, e1_s.at[to], e1_r.at[0], 2 * to + core, band)
 
     def finish(layer, alpha):
         totals = [alpha[0:1] * held[0, k] for k in range(9)]
@@ -384,8 +398,10 @@
             def _():
                 finish(layer, alpha)
 
-        for k in range(15):
-            block_copy(k).start()
+        for to in ORDER:
+            @pl.when(to != depth)
+            def _():
+                block_copy(to).start()
 
     @pl.when(jnp.logical_not(owner))
     def _():
@@ -393,7 +409,6 @@
 
     start = pl.multiple_of(72 * band, 8)
     place = out.at[core, pl.ds(start, 72)]
-    sibling = 2 * depth + 1 - core
     own = pltpu.make_async_copy(block, place, loc_sem.at[0])
     own.start()
 
@@ -442,14 +457,16 @@
             def _():
                 c.wait_send()
     for layer in range(2):
-        @pl.when(m != owners[layer])
+        @pl.when(m != OWNERS[layer])
         def _():
             to_owner(layer).wait_send()
 
     @pl.when(owner)
     def _():
-        for k in range(15):
-            block_copy(k).wait_send()
+        for to in ORDER:
+            @pl.when(to != depth)
+            def _():
+                block_copy(to).wait_send()
 
         @pl.loop(1, 16)
         def _(j):
@@ -482,7 +499,7 @@
             vmem((72, 128), F32),
             dma((3,)), dma((4,)), dma((4,)),
             dma((12,)), dma((12,)), dma((8,)), dma((6,)),
-            dma((2,)), dma((1,)), dma((15,)), dma((1,)), dma((15,)), dma((1,)),
+            dma((2,)), dma((1,)), dma((15,)), dma((1,)), dma((16,)), dma((1,)),
             dma((15,)), dma((15,)), dma((16,)), dma((16,)), dma((1,)),
         ],
         compiler_params=pltpu.CompilerParams(

time: 68.3 us -> 66.3 us (0.971)
  the two profiles are of different devices: /device:TPU:33 before, /device:TPU:1 now
where the time goes in v4:
time: 66.3 us; the launch traced here: 66.1 us
  Pallas kernels  63.6 us (96%)
  other arithmetic  2.46 us (4%)
    pallas_call x1, Pallas kernels, local(): pl.pallas_call(kernel, out_shape=jax.ShapeDtypeStruct((2, 1152, 128), F32...  63.6 us
    broadcast_in_dim x1, other arithmetic, local(): return (filters - rates[:, None, None] * merged)[None]  2.46 us

profile of v4, /device:TPU:1, one launch (start us, length us, event | category | flops | bytes accessed | tf_op | source)
XLA Modules:
  0.0 66.1 jit_solution(12291318643933106503)
XLA Ops:
  0.0 0.0 copy-start
  0.0 0.0 copy-start.1
  0.0 63.6 %adasum_step.1 = f32[2,1152,128]{2,1,0:T(8,128)} custom-call(f32[512,128]{1,0:T(8,128)} %bitcast.4, f32[512,128]{1,0:T(8,128)} %bitcast.5, f32[2,1152,128]{2,1,0:T(8,128)} %fil_in.1), custom_call_target="tpu_custom_call" | custom-call | tf_op jit(solution)/shard_map/adasum_step/pallas_call | solution.py:480
  63.7 0.0 copy-done
  63.7 0.0 copy-done.1
  63.7 2.5 %subtract_bitcast_fusion = f32[1,2,1152,128]{3,2,1,0:T(8,128)} fusion(f32[2,1152,128]{2,1,0:T(8,128)S(1)} %copy-done, f32[2,1152,128]{2,1,0:T(8,128)} %adasum_step.1, f32[2]{0:T(128)S(1)} %copy-done.1), kind=kLoop, calls=%fused_computation | loop fusion | flops 589824 | bytes 3538952 | tf_op jit(solution)/shard_map/broadcast_in_dim | solution.py:510
Async XLA Ops:
  0.0 63.7 %copy-start = (f32[2,1152,128]{2,1,0:T(8,128)S(1)}, f32[2,1152,128]{2,1,0:T(8,128)}, u32[]{:S(2)}) copy-start(f32[2,1152,128]{2,1,0:T(8,128)} %fil_in.1) | copy-start | bytes 3538948
  0.0 63.7 %copy-start.1 = (f32[2]{0:T(128)S(1)}, f32[2]{0:T(128)}, u32[]{:S(2)}) copy-start(f32[2]{0:T(128)} %param.7) | copy-start | bytes 28

commit v5 on v4

--- a/solution.py
+++ b/solution.py
@@ -93,7 +93,7 @@
     return hi, mid, (v - mid.astype(F32)).astype(BF16)
 
 
-OWNERS = (2, 9)
+OWNERS = (4, 7)
 ORDER = (0, 1, 2, 3, 4, 15, 5, 14, 6, 13, 7, 12, 8, 11, 9, 10)
 
 
@@ -479,9 +479,9 @@
     vmem = pltpu.VMEM
     merged = pl.pallas_call(
         kernel,
-        out_shape=jax.ShapeDtypeStruct((2, 1152, 128), F32),
+        out_shape=pltpu.VMEM((2, 1152, 128), F32),
         in_specs=[hbm, hbm, hbm],
-        out_specs=hbm,
+        out_specs=pl.BlockSpec(memory_space=pltpu.VMEM),
         scratch_shapes=[
             vmem((512, 128), F32), vmem((512, 128), F32), vmem((2, 1152, 128), F32),
             *[vmem((2, 128, 128), F32)] * 4,

time: 66.3 us -> 63.8 us (0.962)
  other arithmetic: 2.46 us -> 1.19 us
  Pallas kernels: 63.6 us -> 62.4 us
    broadcast_in_dim x1, other arithmetic: 2.46 us -> 1.19 us  [local(): return (filters - rates[:, None, None] * merged)[None]]
    pallas_call x1, Pallas kernels: 63.6 us -> 62.4 us  [local(): pl.pallas_call(kernel, out_shape=pltpu.VMEM((2, 1152, 128), F32), in_spec...]
where the time goes in v5:
time: 63.8 us; the launch traced here: 63.7 us
  Pallas kernels  62.4 us (98%)
  other arithmetic  1.19 us (2%)
    pallas_call x1, Pallas kernels, local(): pl.pallas_call(kernel, out_shape=pltpu.VMEM((2, 1152, 128), F32), in_spec...  62.4 us

profile of v5, /device:TPU:1, one launch (start us, length us, event | category | flops | bytes accessed | tf_op | source)
XLA Modules:
  0.0 63.7 jit_solution(3688095594004042656)
XLA Ops:
  0.0 0.0 copy-start
  0.0 0.0 copy-start.1
  0.0 62.4 %adasum_step.1 = f32[2,1152,128]{2,1,0:T(8,128)S(1)} custom-call(f32[512,128]{1,0:T(8,128)} %bitcast.4, f32[512,128]{1,0:T(8,128)} %bitcast.5, f32[2,1152,128]{2,1,0:T(8,128)} %fil_in.1), custom_call_target="tpu_custom_call" | custom-call | tf_op jit(solution)/shard_map/adasum_step/pallas_call | solution.py:480
  62.4 0.0 copy-done
  62.5 0.0 copy-done.1
  62.5 1.2 %subtract_bitcast_fusion = f32[1,2,1152,128]{3,2,1,0:T(8,128)} fusion(f32[2,1152,128]{2,1,0:T(8,128)S(1)} %copy-done, f32[2,1152,128]{2,1,0:T(8,128)S(1)} %adasum_step.1, f32[2]{0:T(128)S(1)} %copy-done.1), kind=kLoop, calls=%fused_computation | loop fusion | flops 589824 | bytes 3538952 | tf_op jit(solution)/shard_map/broadcast_in_dim | solution.py:510
Async XLA Ops:
  0.0 62.4 %copy-start = (f32[2,1152,128]{2,1,0:T(8,128)S(1)}, f32[2,1152,128]{2,1,0:T(8,128)}, u32[]{:S(2)}) copy-start(f32[2,1152,128]{2,1,0:T(8,128)} %fil_in.1) | copy-start | bytes 3538948
  0.0 62.5 %copy-start.1 = (f32[2]{0:T(128)S(1)}, f32[2]{0:T(128)}, u32[]{:S(2)}) copy-start(f32[2]{0:T(128)} %param.7) | copy-start | bytes 28

commit v6 on v5

--- a/solution.py
+++ b/solution.py
@@ -93,7 +93,11 @@
     return hi, mid, (v - mid.astype(F32)).astype(BF16)
 
 
-OWNERS = (4, 7)
+OWNERS = (0, 9)
+STEPS = tuple(sorted(
+    ((dy, dx) for dy in range(4) for dx in range(4) if dy or dx),
+    key=lambda step: -sum(min(d, 4 - d) for d in step),
+))
 ORDER = (0, 1, 2, 3, 4, 15, 5, 14, 6, 13, 7, 12, 8, 11, 9, 10)
 
 
@@ -143,14 +147,10 @@
     for c in loads:
         c.start()
 
-    for c, field, edge, vh, vl in ((loads[0], img, xedge, xh, xl), (loads[1], cot, yedge, yh, yl)):
+    for c, field, edge in ((loads[0], img, xedge), (loads[1], cot, yedge)):
         c.wait()
-        for r in range(4):
-            v = field[pl.ds(r, 128, stride=4), :]
-            if r % 3 == 0:
-                edge[r // 3] = v
-            cols = slice(128 * (r + 1), 128 * (r + 2))
-            vh[:, cols], vl[:, cols] = halves(v)
+        edge[0] = field[pl.ds(0, 128, stride=4), :]
+        edge[1] = field[pl.ds(3, 128, stride=4), :]
 
     def halo(edge, landing, k, up):
         if up:
@@ -181,6 +181,11 @@
     @pl.when(band < 15)
     def _():
         halo(yedge, yhalo, 3, False).start()
+
+    for field, vh, vl in ((img, xh, xl), (cot, yh, yl)):
+        for r in range(4):
+            cols = slice(128 * (r + 1), 128 * (r + 2))
+            vh[:, cols], vl[:, cols] = halves(field[pl.ds(r, 128, stride=4), :])
 
     loads[2].wait()
     for a in range(3):
@@ -306,18 +311,22 @@
         return copies
 
     def pass_on(layer, g):
-        for c in first_copies(layer, g):
-            c.wait_recv()
-        sum_x[layer] = g[:, :, x_odd, x_half, x_odd] + (
-            along_x[layer, 0] + (along_x[layer, 1] + along_x[layer, 2])
-        )
-        sum_y[layer] = g[:, y_half, y_odd, :, 1 - y_odd] + (
-            along_y[layer, 0] + (along_y[layer, 1] + along_y[layer, 2])
-        )
-        for going, c in last_copies(layer):
-            @pl.when(going)
-            def _():
-                c.start()
+        arriving, leaving = first_copies(layer, g), last_copies(layer)
+        for route in range(2):
+            for c in arriving[route::2]:
+                c.wait_recv()
+            if route == 0:
+                sum_x[layer] = g[:, :, x_odd, x_half, x_odd] + (
+                    along_x[layer, 0] + (along_x[layer, 1] + along_x[layer, 2])
+                )
+            else:
+                sum_y[layer] = g[:, y_half, y_odd, :, 1 - y_odd] + (
+                    along_y[layer, 0] + (along_y[layer, 1] + along_y[layer, 2])
+                )
+            for going, c in leaving[route::2]:
+                @pl.when(going)
+                def _():
+                    c.start()
 
     def take(layer):
         for slot in range(3):
@@ -355,89 +364,6 @@
     hand_over(1)
     take(0)
     hand_over(0)
-
-    def gram_copy(j):
-        return remote(gram_b.at[band], gram_b.at[band], d_s.at[j - 1], d_r.at[0], m, (band + j) % 16)
-
-    def block_copy(to):
-        return remote(block, block, e1_s.at[to], e1_r.at[0], 2 * to + core, band)
-
-    def finish(layer, alpha):
-        totals = [alpha[0:1] * held[0, k] for k in range(9)]
-        for q in range(1, 32):
-            totals = [v + alpha[q : q + 1] * held[q, k] for k, v in enumerate(totals)]
-        for k, v in enumerate(totals):
-            t = k if layer == 0 else 3 * (k % 3) + k // 3
-            block[pl.ds(t, 8, stride=9), :] = v
-
-    @pl.when(owner)
-    def _():
-        pltpu.make_async_copy(held.at[pl.ds(0, 31)], held.at[pl.ds(0, 31)], c_r.at[0]).wait()
-        flat = held.reshape(2304, 128)
-        total = jnp.zeros((96, 96), F32)
-        for row in range(0, 72, 4):
-            lines = [flat[pl.ds(row + q, 32, stride=72), :] for q in range(4)]
-            v = jnp.concatenate(thirds(jnp.concatenate(lines, axis=1)), axis=0)
-            total = total + nt(v, v)
-        total = total[0:32] + total[32:64] + total[64:96]
-        total = total[:, 0:32] + total[:, 32:64] + total[:, 64:96]
-        gram_b[band] = jnp.concatenate([total[8 * q : 8 * q + 8] for q in range(4)], axis=1)
-
-        @pl.loop(1, 16)
-        def _(j):
-            gram_copy(j).start()
-
-        pltpu.make_async_copy(gram_b.at[pl.ds(0, 15)], gram_b.at[pl.ds(0, 15)], d_r.at[0]).wait()
-        packed = jnp.sum(gram_b[...], axis=0)
-        rows = [packed if q == 0 else pltpu.roll(packed, 128 - 32 * q, 1) for q in range(4)]
-        gram = jnp.concatenate(rows, axis=0)
-        lane = lax.broadcasted_iota(jnp.int32, gram.shape, 1)
-        alpha = adasum_weights(jnp.where(lane < 32, gram, 0.0))
-        for layer in range(2):
-            @pl.when(core == layer)
-            def _():
-                finish(layer, alpha)
-
-        for to in ORDER:
-            @pl.when(to != depth)
-            def _():
-                block_copy(to).start()
-
-    @pl.when(jnp.logical_not(owner))
-    def _():
-        pltpu.make_async_copy(block, block, e1_r.at[0]).wait()
-
-    start = pl.multiple_of(72 * band, 8)
-    place = out.at[core, pl.ds(start, 72)]
-    own = pltpu.make_async_copy(block, place, loc_sem.at[0])
-    own.start()
-
-    @pl.loop(1, 16)
-    def _(j):
-        remote(block, place, e2_s.at[j - 1], e2_r.at[j - 1], m, (band + j) % 16).start()
-
-    remote(block, place, f_s.at[0], f_r.at[0], sibling, band).start()
-
-    @pl.loop(1, 16)
-    def _(j):
-        source = (band + 16 - j) % 16
-        there = out.at[core, pl.ds(pl.multiple_of(72 * source, 8), 72)]
-        remote(block, there, e2_s.at[j - 1], e2_r.at[j - 1], m, band).wait_recv()
-        remote(there, there, f_s.at[j], f_r.at[j], sibling, band).start()
-
-    @pl.loop(0, 16)
-    def _(j):
-        source = (band + 16 - j) % 16
-        there = out.at[1 - core, pl.ds(pl.multiple_of(72 * source, 8), 72)]
-        copy = remote(block, there, f_s.at[j], f_r.at[j], sibling, band)
-        copy.wait_recv()
-        copy.wait_send()
-
-    own.wait()
-
-    @pl.loop(1, 16)
-    def _(j):
-        remote(block, place, e2_s.at[j - 1], e2_r.at[j - 1], m, band).wait_send()
 
     @pl.when(band > 0)
     def _():
@@ -461,6 +387,89 @@
         def _():
             to_owner(layer).wait_send()
 
+    def peer(dy, dx):
+        return ((y + dy + 4) % 4) * 4 + (x + dx + 4) % 4
+
+    def gram_copy(k):
+        return remote(gram_b.at[band], gram_b.at[band], d_s.at[k], d_r.at[0], m, peer(*STEPS[k]))
+
+    def block_copy(to):
+        return remote(block, block, e1_s.at[to], e1_r.at[0], 2 * to + core, band)
+
+    def finish(layer, alpha):
+        totals = [alpha[0:1] * held[0, k] for k in range(9)]
+        for q in range(1, 32):
+            totals = [v + alpha[q : q + 1] * held[q, k] for k, v in enumerate(totals)]
+        for k, v in enumerate(totals):
+            t = k if layer == 0 else 3 * (k % 3) + k // 3
+            block[pl.ds(t, 8, stride=9), :] = v
+
+    @pl.when(owner)
+    def _():
+        pltpu.make_async_copy(held.at[pl.ds(0, 31)], held.at[pl.ds(0, 31)], c_r.at[0]).wait()
+        flat = held.reshape(2304, 128)
+        total = jnp.zeros((96, 96), F32)
+        for row in range(0, 72, 4):
+            lines = [flat[pl.ds(row + q, 32, stride=72), :] for q in range(4)]
+            v = jnp.concatenate(thirds(jnp.concatenate(lines, axis=1)), axis=0)
+            total = total + nt(v, v)
+        total = total[0:32] + total[32:64] + total[64:96]
+        total = total[:, 0:32] + total[:, 32:64] + total[:, 64:96]
+        gram_b[band] = jnp.concatenate([total[8 * q : 8 * q + 8] for q in range(4)], axis=1)
+
+        for k in range(15):
+            gram_copy(k).start()
+
+        pltpu.make_async_copy(gram_b.at[pl.ds(0, 15)], gram_b.at[pl.ds(0, 15)], d_r.at[0]).wait()
+        packed = jnp.sum(gram_b[...], axis=0)
+        rows = [packed if q == 0 else pltpu.roll(packed, 128 - 32 * q, 1) for q in range(4)]
+        gram = jnp.concatenate(rows, axis=0)
+        lane = lax.broadcasted_iota(jnp.int32, gram.shape, 1)
+        alpha = adasum_weights(jnp.where(lane < 32, gram, 0.0))
+        for layer in range(2):
+            @pl.when(core == layer)
+            def _():
+                finish(layer, alpha)
+
+        for to in ORDER:
+            @pl.when(to != depth)
+            def _():
+                block_copy(to).start()
+
+    @pl.when(jnp.logical_not(owner))
+    def _():
+        pltpu.make_async_copy(block, block, e1_r.at[0]).wait()
+
+    start = pl.multiple_of(72 * band, 8)
+    place = out.at[core, pl.ds(start, 72)]
+    own = pltpu.make_async_copy(block, place, loc_sem.at[0])
+    own.start()
+
+    def rows_of(layer, source):
+        return out.at[layer, pl.ds(pl.multiple_of(72 * source, 8), 72)]
+
+    def to_band(k, dy, dx):
+        return remote(block, place, e2_s.at[k], e2_r.at[k], m, peer(dy, dx))
+
+    for k, (dy, dx) in enumerate(STEPS):
+        to_band(k, dy, dx).start()
+    remote(block, place, f_s.at[15], f_r.at[15], sibling, band).start()
+
+    for k, (dy, dx) in enumerate(STEPS):
+        there = rows_of(core, peer(-dy, -dx))
+        remote(block, there, e2_s.at[k], e2_r.at[k], m, band).wait_recv()
+        remote(there, there, f_s.at[k], f_r.at[k], sibling, band).start()
+
+    for k, (dy, dx) in enumerate((*STEPS, (0, 0))):
+        there = rows_of(1 - core, peer(-dy, -dx))
+        copy = remote(block, there, f_s.at[k], f_r.at[k], sibling, band)
+        copy.wait_recv()
+        copy.wait_send()
+
+    own.wait()
+    for k, (dy, dx) in enumerate(STEPS):
+        to_band(k, dy, dx).wait_send()
+
     @pl.when(owner)
     def _():
         for to in ORDER:
@@ -468,9 +477,8 @@
             def _():
                 block_copy(to).wait_send()
 
-        @pl.loop(1, 16)
-        def _(j):
-            gram_copy(j).wait_send()
+        for k in range(15):
+            gram_copy(k).wait_send()
 
 
 def local(images, cotangent, filters, rates):

time: 63.8 us -> 63.1 us (0.989)
  Pallas kernels: 62.4 us -> 61.7 us
    pallas_call x1, Pallas kernels: 62.4 us -> 61.7 us  [local(): pl.pallas_call(kernel, out_shape=pltpu.VMEM((2, 1152, 128), F32), in_spec...]
where the time goes in v6:
time: 63.1 us; the launch traced here: 63 us
  Pallas kernels  61.7 us (98%)
  other arithmetic  1.19 us (2%)
    pallas_call x1, Pallas kernels, local(): pl.pallas_call(kernel, out_shape=pltpu.VMEM((2, 1152, 128), F32), in_spec...  61.7 us

profile of v6, /device:TPU:1, one launch (start us, length us, event | category | flops | bytes accessed | tf_op | source)
XLA Modules:
  0.0 63.0 jit_solution(11041728008459701542)
XLA Ops:
  0.0 0.0 copy-start
  0.0 0.0 copy-start.1
  0.0 61.7 %adasum_step.1 = f32[2,1152,128]{2,1,0:T(8,128)S(1)} custom-call(f32[512,128]{1,0:T(8,128)} %bitcast.4, f32[512,128]{1,0:T(8,128)} %bitcast.5, f32[2,1152,128]{2,1,0:T(8,128)} %fil_in.1), custom_call_target="tpu_custom_call" | custom-call | tf_op jit(solution)/shard_map/adasum_step/pallas_call | solution.py:488
  61.7 0.0 copy-done
  61.8 0.0 copy-done.1
  61.8 1.2 %subtract_bitcast_fusion = f32[1,2,1152,128]{3,2,1,0:T(8,128)} fusion(f32[2,1152,128]{2,1,0:T(8,128)S(1)} %copy-done, f32[2,1152,128]{2,1,0:T(8,128)S(1)} %adasum_step.1, f32[2]{0:T(128)S(1)} %copy-done.1), kind=kLoop, calls=%fused_computation | loop fusion | flops 589824 | bytes 3538952 | tf_op jit(solution)/shard_map/broadcast_in_dim | solution.py:518
Async XLA Ops:
  0.0 61.7 %copy-start = (f32[2,1152,128]{2,1,0:T(8,128)S(1)}, f32[2,1152,128]{2,1,0:T(8,128)}, u32[]{:S(2)}) copy-start(f32[2,1152,128]{2,1,0:T(8,128)} %fil_in.1) | copy-start | bytes 3538948
  0.0 61.8 %copy-start.1 = (f32[2]{0:T(128)S(1)}, f32[2]{0:T(128)}, u32[]{:S(2)}) copy-start(f32[2]{0:T(128)} %param.7) | copy-start | bytes 28

commit v7 on v6

--- a/solution.py
+++ b/solution.py
@@ -275,7 +275,7 @@
 
     def first_copies(layer, g):
         copies = []
-        for step in (1, 2, 3):
+        for step in (2, 1, 3):
             to = (x + step) % 4
             k = 6 * layer + step - 1
             copies.append(

time: 63.1 us -> 62.9 us (level)
  no operation moved by 1% of the time
where the time goes in v7:
time: 62.9 us; the launch traced here: 62.8 us
  Pallas kernels  61.6 us (98%)
  other arithmetic  1.19 us (2%)
    pallas_call x1, Pallas kernels, local(): pl.pallas_call(kernel, out_shape=pltpu.VMEM((2, 1152, 128), F32), in_spec...  61.6 us

profile of v7, /device:TPU:1, one launch (start us, length us, event | category | flops | bytes accessed | tf_op | source)
XLA Modules:
  0.0 62.8 jit_solution(2118183877463044391)
XLA Ops:
  0.0 0.0 copy-start
  0.0 0.0 copy-start.1
  0.0 61.6 %adasum_step.1 = f32[2,1152,128]{2,1,0:T(8,128)S(1)} custom-call(f32[512,128]{1,0:T(8,128)} %bitcast.4, f32[512,128]{1,0:T(8,128)} %bitcast.5, f32[2,1152,128]{2,1,0:T(8,128)} %fil_in.1), custom_call_target="tpu_custom_call" | custom-call | tf_op jit(solution)/shard_map/adasum_step/pallas_call | solution.py:488
  61.6 0.0 copy-done
  61.6 0.0 copy-done.1
  61.6 1.2 %subtract_bitcast_fusion = f32[1,2,1152,128]{3,2,1,0:T(8,128)} fusion(f32[2,1152,128]{2,1,0:T(8,128)S(1)} %copy-done, f32[2,1152,128]{2,1,0:T(8,128)S(1)} %adasum_step.1, f32[2]{0:T(128)S(1)} %copy-done.1), kind=kLoop, calls=%fused_computation | loop fusion | flops 589824 | bytes 3538952 | tf_op jit(solution)/shard_map/broadcast_in_dim | solution.py:518
Async XLA Ops:
  0.0 61.6 %copy-start = (f32[2,1152,128]{2,1,0:T(8,128)S(1)}, f32[2,1152,128]{2,1,0:T(8,128)}, u32[]{:S(2)}) copy-start(f32[2,1152,128]{2,1,0:T(8,128)} %fil_in.1) | copy-start | bytes 3538948
  0.0 61.6 %copy-start.1 = (f32[2]{0:T(128)S(1)}, f32[2]{0:T(128)}, u32[]{:S(2)}) copy-start(f32[2]{0:T(128)} %param.7) | copy-start | bytes 28
